TPU v7x, 512 devices: a whole 4x8x8 slice. The times are simulated.
512 devices in a mesh: fsdp: 64 (over y, z), tp: 8 (over x, core).
Axes of the slice: x: 4, y: 8, z: 8, core: 2. Of those that a mesh axis runs over, the one named last changes fastest.
Arguments:
- momentum: bfloat16 [8192, 28672], P('fsdp', 'tp'), may hold values from -6 to 6
- gradient: bfloat16 [8192, 28672], P('fsdp', 'tp'), may hold values from -6 to 6
- basis_rows: bfloat16 [256, 28672], P('fsdp', 'tp'), may hold values from -0.03125 to 0.03125
Outputs:
- new_momentum: bfloat16 [8192, 28672], P('fsdp', 'tp')
- new_basis: bfloat16 [256, 28672], P('fsdp', 'tp')
- update: bfloat16 [8192, 28672], P('fsdp', 'tp')
All inputs are finite; a program needn't handle non-finite values.
Results may differ from a plain program's by a relative error of at most 0.017.
Values may be sent and summed in bfloat16 or wider, within the bound.
A program may use at most 64 MiB of HBM per device.

v0:
```python
import math

import jax
import jax.numpy as jnp
from jax import lax
from jax.sharding import PartitionSpec as P

D = 8192
FF = 28672
RANK = 256


epsilon = 1e-06
momentum_decay = 0.95


def local(momentum, gradient, basis_rows):
    buffer = (momentum.astype(jnp.float32) + gradient.astype(jnp.float32)).astype(jnp.bfloat16)
    partial_proj = lax.dot_general(
        buffer,
        lax.all_gather(basis_rows, "fsdp", axis=0, tiled=True),
        (((1,), (1,)), ((), ())),
        preferred_element_type=jnp.float32,
    )
    projected = lax.psum(partial_proj, "tp")
    gram_matrix = lax.psum(jnp.dot(projected.T, projected, precision=lax.Precision.HIGHEST), "fsdp")
    lower_factor = jnp.linalg.cholesky(gram_matrix)
    orthonormal = lax.linalg.triangular_solve(
        lower_factor, projected, left_side=False, lower=True, transpose_a=True
    )
    ortho_low = orthonormal.astype(jnp.bfloat16)
    own_rows = basis_rows.shape[0]
    partial_back = lax.dot_general(
        ortho_low, buffer, (((0,), (0,)), ((), ())), preferred_element_type=jnp.float32
    )
    back_factor = lax.psum(partial_back, "fsdp")
    column_squares = lax.psum(jnp.sum(back_factor * back_factor, axis=1), "tp")
    full_basis = (back_factor * lax.rsqrt(column_squares + epsilon)[:, None]).astype(jnp.bfloat16)
    row_scale = jnp.sqrt(column_squares + epsilon).astype(jnp.bfloat16)
    own_basis = lax.dynamic_slice_in_dim(full_basis, lax.axis_index("fsdp") * own_rows, own_rows, 0)
    scaled_ortho = (ortho_low.astype(jnp.float32) * row_scale.astype(jnp.float32)[None, :]).astype(
        jnp.bfloat16
    )
    new_momentum = (
        buffer.astype(jnp.float32)
        - (1.0 - momentum_decay)
        * jnp.dot(scaled_ortho, full_basis, preferred_element_type=jnp.float32)
    ).astype(jnp.bfloat16)
    unit_scale = math.sqrt(D * FF / RANK)
    update = (
        unit_scale * jnp.dot(ortho_low, full_basis, preferred_element_type=jnp.float32)
    ).astype(jnp.bfloat16)
    return (new_momentum, own_basis, update)


def solution(mesh):
    return jax.shard_map(
        local,
        mesh=mesh,
        in_specs=(P("fsdp", "tp"), P("fsdp", "tp"), P("fsdp", "tp")),
        out_specs=(P("fsdp", "tp"), P("fsdp", "tp"), P("fsdp", "tp")),
        check_vma=False,
    )
```

profile of v0, /device:TPU:1, one launch (start us, length us, event | category | flops | bytes accessed | tf_op | source)
XLA Modules:
  0.0 586.7 jit_solution(17672266101809818297)
XLA Ops:
  7.2 0.7 all-gather.3.cloned.1.call-update
  8.0 87.7 %all-gather.3.cloned.1.call-done = bf16[64,4,3584]{2,1,0:T(4,128)(2,1)} async-done(((bf16[1,4,3584]{2,1,0:T(4,128)(2,1)}), bf16[64,4,3584]{2,1,0:T(4,128)(2,1)}) %all-gather.3.cloned.1.call-update) | async-done | bytes 1835024 | tf_op jit(solution)/shard_map/all_gather | solution.py:21
  95.6 3.9 reshape.45
  99.5 2.9 fusion.16
  102.5 69.7 %all-reduce.5.cloned.1.call-done = f32[128,256]{1,0:T(8,128)} async-done(((f32[128,256]{1,0:T(8,128)}), f32[128,256]{1,0:T(8,128)}) %all-reduce.5.cloned.1.call-update) | async-done | bytes 131088 | tf_op jit(solution)/shard_map/psum | solution.py:25
  172.3 2.1 fusion.19
  174.4 150.4 %all-reduce.7.cloned.1.call-done = f32[256,256]{0,1:T(8,128)} async-done(((f32[256,256]{0,1:T(8,128)}), f32[256,256]{0,1:T(8,128)}) %all-reduce.7.cloned.1.call-update) | async-done | bytes 262160 | tf_op jit(solution)/shard_map/psum | solution.py:26
  324.8 1.1 copy.9
  325.9 1.0 fusion.3
  327.0 11.7 %cholesky.50 = f32[128,128]{1,0:T(8,128)S(1)} custom-call(f32[128,128]{1,0:T(8,128)S(1)} %cholesky.118), custom_call_target="Cholesky" | custom-call | tf_op jit(solution)/shard_map/jit(cholesky)/cholesky | solution.py:27
  338.7 9.8 %custom-call.14 = f32[1,128,128]{1,2,0:T(8,128)S(1)} custom-call(f32[1,128,128]{2,1,0:T(8,128)S(1)} %get-tuple-element.24), custom_call_target="InvertDiagBlocksLowerTriangular" | custom-call | tf_op jit(solution)/shard_map/jit(cholesky)/cholesky | solution.py:27
  348.5 0.2 constant_dynamic-update-slice_fusion
  348.8 0.3 convolution_subtract_fusion.1
  349.0 11.7 %cholesky.105 = f32[128,128]{1,0:T(8,128)S(1)} custom-call(f32[128,128]{1,0:T(8,128)S(1)} %convolution_subtract_fusion.1), custom_call_target="Cholesky" | custom-call | tf_op jit(solution)/shard_map/jit(cholesky)/cholesky | solution.py:27
  360.8 0.6 compare_reduce_fusion
  362.8 4.1 while.1
  363.0 0.6 fusion.30
  363.6 1.4 bitcast_dynamic-update-slice_fusion.2
  365.0 0.6 fusion.30
  365.6 1.4 bitcast_dynamic-update-slice_fusion.2
  367.0 19.7 %custom-call.15 = f32[2,128,128]{1,2,0:T(8,128)S(1)} custom-call(f32[2,128,128]{2,1,0:T(8,128)S(1)} %get-tuple-element.10), custom_call_target="InvertDiagBlocksLowerTriangular" | custom-call | tf_op jit(solution)/shard_map/triangular_solve | solution.py:28
  386.7 0.3 fusion.18
  387.0 0.3 convolution_subtract_fusion
  387.2 0.3 convolution_convert_fusion
  387.5 2.5 fusion.11
  390.1 165.4 %all-reduce.9.cloned.1.call-done = f32[256,3584]{1,0:T(8,128)} async-done(((f32[256,3584]{1,0:T(8,128)}), f32[256,3584]{1,0:T(8,128)}) %all-reduce.9.cloned.1.call-update) | async-done | bytes 3670032 | tf_op jit(solution)/shard_map/psum | solution.py:36
  555.5 2.4 multiply_reduce_fusion
  557.8 16.4 %psum.31 = f32[256]{0:T(256)S(1)} all-reduce(f32[256]{0:T(256)S(1)} %multiply_reduce_fusion), channel_id=1, replica_groups=mesh['fsdp'=64,'tp'=8] {'tp'}, use_global_device_ids=true, to_apply=%region_8.9 | all-reduce | flops 256 | bytes 2048 | tf_op jit(solution)/shard_map/psum | solution.py:37
  574.2 2.4 multiply_convert_fusion
  576.6 1.4 fusion.2
  578.0 1.6 fusion.1
  579.6 0.6 constant_dynamic-slice_fusion.1
  (24 shorter events, 0.4 us)
Async XLA Ops:
  7.2 88.5 %all-gather.3.cloned.1.call-start = ((), (), s32[]{:S(2)}) async-start(), calls=%async_computation.3 | async-start | bytes 1863680 | tf_op jit(solution)/shard_map/all_gather | solution.py:21
  7.9 91.6 %copy-start = (bf16[128,3584]{1,0:T(8,128)(2,1)S(1)}, bf16[128,3584]{1,0:T(8,128)(2,1)}, u32[]{:S(2)}) copy-start(bf16[128,3584]{1,0:T(8,128)(2,1)} %param.4) | copy-start | bytes 2752516
  7.9 91.6 %copy-start.1 = (bf16[128,3584]{1,0:T(8,128)(2,1)S(1)}, bf16[128,3584]{1,0:T(8,128)(2,1)}, u32[]{:S(2)}) copy-start(bf16[128,3584]{1,0:T(8,128)(2,1)} %param.3) | copy-start | bytes 2752516
  7.9 164.3 %all-reduce.5.cloned.1.call-start = ((), (), s32[]{:S(2)}) async-start(), calls=%async_computation | async-start | bytes 262144 | tf_op jit(solution)/shard_map/psum | solution.py:25
  102.5 222.4 %all-reduce.7.cloned.1.call-start = ((), (), s32[]{:S(2)}) async-start(), calls=%async_computation.1 | async-start | bytes 524288 | tf_op jit(solution)/shard_map/psum | solution.py:26
  174.4 381.1 %all-reduce.9.cloned.1.call-start = ((), (), s32[]{:S(2)}) async-start(), calls=%async_computation.2 | async-start | bytes 7340032 | tf_op jit(solution)/shard_map/psum | solution.py:36
  325.9 60.7 %copy-start.2 = (f32[128,256]{1,0:T(8,128)S(1)}, f32[128,256]{1,0:T(8,128)}, u32[]{:S(2)}) copy-start(f32[128,256]{1,0:T(8,128)} %all-reduce.5.cloned.1.call-done) | copy-start | bytes 393220
Sparse Core Ops, SparseCore 0:
  11.1 84.5 all-gather.2
  102.6 69.6 all-reduce.4
  176.4 148.4 all-reduce.6
  390.2 165.2 all-reduce.8
where the time goes:
time: 587 us
  waiting for transfers between devices  474 us (81%)
  other arithmetic  59.4 us (10%)
  blocking collectives  16.4 us (3%)
  between operations  15.2 us (3%)
  matrix products  11.7 us (2%)
  local copies, waits for them, and re-layouts  9.67 us (2%)
    psum x1, waiting for transfers between devices, local(): back_factor = lax.psum(partial_back, 'fsdp')  165 us
    psum x1, waiting for transfers between devices, local(): lax.psum(jnp.dot(projected.T, projected, precision=lax.Precision.HIGHEST)...  150 us
    all_gather x1, waiting for transfers between devices, local(): lax.all_gather(basis_rows, 'fsdp', axis=0, tiled=True)  87.7 us
    psum x1, waiting for transfers between devices, local(): projected = lax.psum(partial_proj, 'tp')  69.7 us
    another operation x6, other arithmetic, local(): lower_factor = jnp.linalg.cholesky(gram_matrix)  34 us
    another operation x3, other arithmetic, local(): lax.linalg.triangular_solve(lower_factor, projected, left_side=False, low...  19.7 us
    psum x1, blocking collectives, local(): column_squares = lax.psum(jnp.sum(back_factor * back_factor, axis=1), 'tp')  16.4 us
  transfers between devices with their start and end apart: 4, of which 4 were waited for; matrix products, arithmetic and copies ran while one was open for 0% of the time, Pallas kernels for 0%

commit v1 on v0

v1 whole, which is shorter than its diff:
```python
import functools
import math

import jax
import jax.numpy as jnp
from jax import lax
from jax.experimental import pallas as pl
from jax.experimental.pallas import tpu as pltpu
from jax.sharding import PartitionSpec as P

D = 8192
FF = 28672
RANK = 256
NY = 8
NZ = 8
NF = 64
NT = 8
ROWS = D // NF
COLS = FF // NT
OWN = RANK // NF
PARTS = 4
PC = COLS // PARTS
SLOT = 16

epsilon = 1e-06
momentum_decay = 0.95
UNIT = math.sqrt(D * FF / RANK)

F32 = jnp.float32
BF16 = jnp.bfloat16
MESH = pl.DeviceIdType.MESH
HIGHEST = lax.Precision.HIGHEST


def mod8(v):
    return lax.rem(v + 16, 8)


def place():
    f = lax.axis_index("fsdp")
    t = lax.axis_index("tp")
    y = f // NZ
    z = lax.rem(f, NZ)
    even = lax.rem(y + z, 2) == 0
    return f, t, y, z, even


def line(even, y, z, k):
    along_y = jnp.where(even, k, 0)
    along_z = jnp.where(even, 0, k)
    return mod8(y + along_y) * NZ + mod8(z + along_z)


def own_slot(even, y, z):
    return jnp.where(even, z * 4 + y // 2, 32 + y * 4 + z // 2)


def rows_of(slot, count=1):
    return pl.ds(pl.multiple_of(slot * SLOT, SLOT), count * SLOT)


def greet(f, t, y, z):
    barrier = pltpu.get_barrier_semaphore()
    for k in range(1, 8):
        pl.semaphore_signal(barrier, inc=1, device_id=(mod8(y + k) * NZ + z, t), device_id_type=MESH)
        pl.semaphore_signal(barrier, inc=1, device_id=(y * NZ + mod8(z + k), t), device_id_type=MESH)
        pl.semaphore_signal(barrier, inc=1, device_id=(f, mod8(t + k)), device_id_type=MESH)
    pl.semaphore_wait(barrier, 21)


def hops_of(d, c):
    return 4 if d == c else 3


STREAMS = [(ax, d, c) for c in range(2) for ax in range(2) for d in range(2)]


def chunk(ax, origin, c):
    return rows_of(ax * 32 + origin * 4 + c * 2, 2)


def gather(buf, f, t, y, z, even, s1, r1, s2, r2):
    me = own_slot(even, y, z)
    here = jnp.where(even, y // 2, 4 + z // 2)
    for k in (4, 3, 5, 2, 6, 1, 7):
        pltpu.make_async_remote_copy(
            src_ref=buf.at[rows_of(me)],
            dst_ref=buf.at[rows_of(me)],
            send_sem=s1.at[k],
            recv_sem=r1.at[here],
            device_id=(line(even, y, z, k), t),
            device_id_type=MESH,
        ).start()

    def arrival(ax, i):
        slot = jnp.where(ax == 0, z * 4 + i, 32 + y * 4 + i)

        @pl.when(slot != me)
        def _():
            pltpu.make_async_remote_copy(
                src_ref=buf.at[rows_of(slot)],
                dst_ref=buf.at[rows_of(slot)],
                send_sem=s1.at[0],
                recv_sem=r1.at[ax * 4 + i],
                device_id=(f, mod8(t + 1)),
                device_id_type=MESH,
            ).wait_recv()

    def hop(ax, d, c, h):
        step = 1 if d == 0 else -1
        pos = z if ax == 0 else y
        origin = mod8(pos - step * h)
        to = (y * NZ + mod8(z + step)) if ax == 0 else (mod8(y + step) * NZ + z)
        return pltpu.make_async_remote_copy(
            src_ref=buf.at[chunk(ax, origin, c)],
            dst_ref=buf.at[chunk(ax, origin, c)],
            send_sem=s2.at[ax, d, c, h],
            recv_sem=r2.at[ax, d, c, h],
            device_id=(to, t),
            device_id_type=MESH,
        )

    def landed(ax, d, c, h):
        step = 1 if d == 0 else -1
        pos = z if ax == 0 else y
        origin = mod8(pos - step * (h + 1))
        pltpu.make_async_remote_copy(
            src_ref=buf.at[chunk(ax, origin, c)],
            dst_ref=buf.at[chunk(ax, origin, c)],
            send_sem=s2.at[ax, d, c, h],
            recv_sem=r2.at[ax, d, c, h],
            device_id=(f, mod8(t + 1)),
            device_id_type=MESH,
        ).wait_recv()

    sent = []
    for c in range(2):
        for ax in range(2):
            for i in (2 * c, 2 * c + 1):
                arrival(ax, i)
            for d in range(2):
                copy = hop(ax, d, c, 0)
                copy.start()
                sent.append(copy)
    for h in range(4):
        for ax, d, c in STREAMS:
            if h < hops_of(d, c):
                landed(ax, d, c, h)
                if h + 1 < hops_of(d, c):
                    copy = hop(ax, d, c, h + 1)
                    copy.start()
                    sent.append(copy)

    def finish():
        for k in range(1, 8):
            pltpu.make_async_remote_copy(
                src_ref=buf.at[rows_of(me)],
                dst_ref=buf.at[rows_of(me)],
                send_sem=s1.at[k],
                recv_sem=r1.at[here],
                device_id=(f, mod8(t + 1)),
                device_id_type=MESH,
            ).wait_send()
        for copy in sent:
            copy.wait_send()

    return finish


def exchange(src_of, dst_of, ids, pos, send, recv):
    copies = []
    for k in (4, 3, 5, 2, 6, 1, 7):
        p = mod8(pos + k)
        copy = pltpu.make_async_remote_copy(
            src_ref=src_of(p),
            dst_ref=dst_of(pos),
            send_sem=send.at[k],
            recv_sem=recv.at[8 - k],
            device_id=ids(p),
            device_id_type=MESH,
        )
        copy.start()
        copies.append(copy)
    return copies


def arrived(dst_of, ids, pos, send, recv):
    for k in range(1, 8):
        p = mod8(pos + k)
        pltpu.make_async_remote_copy(
            src_ref=dst_of(p),
            dst_ref=dst_of(p),
            send_sem=send.at[k],
            recv_sem=recv.at[k],
            device_id=ids(p),
            device_id_type=MESH,
        ).wait_recv()


def project_kernel(
    m_ref, g_ref, basis_ref, proj_ref, gram_ref,
    vbuf, bbuf, mbuf, gbuf, stage, sel, part, tbuf, gpart, ybuf, zbuf,
    local_sem, s1, r1, s2, r2, ps, pr, as_, ar, ys, yr, zs, zr, bs, br, ts, tr,
):
    f, t, y, z, even = place()
    me = own_slot(even, y, z)
    cm = pltpu.make_async_copy(m_ref, mbuf, local_sem.at[0])
    cg = pltpu.make_async_copy(g_ref, gbuf, local_sem.at[1])
    cb = pltpu.make_async_copy(basis_ref, stage, local_sem.at[2])
    cb.start()
    cm.start()
    cg.start()
    cb.wait()
    own = stage[...].astype(F32)
    pieces = [own[:, j * PC:(j + 1) * PC] for j in range(PARTS)]
    vbuf[rows_of(me), :] = jnp.concatenate(pieces, axis=0).astype(BF16)
    greet(f, t, y, z)
    finish = gather(vbuf, f, t, y, z, even, s1, r1, s2, r2)
    cm.wait()
    cg.wait()
    for j in range(PARTS):
        cols = slice(j * PC, (j + 1) * PC)
        bbuf[:, cols] = (mbuf[:, cols].astype(F32) + gbuf[:, cols].astype(F32)).astype(BF16)

    def choose(i, carry):
        base = pl.multiple_of(i * 128, 128)
        row = base + lax.broadcasted_iota(jnp.int32, (128, RANK), 0)
        slot = row // SLOT
        first, second = (slot // 4) % 8, slot % 4
        zf = first
        yf = 2 * second + (first % 2)
        yo = first
        zo = 2 * second + (1 - first % 2)
        dev = jnp.where(slot < 32, yf * NZ + zf, yo * NZ + zo)
        rank = dev * OWN + row % 4
        hit = rank == lax.broadcasted_iota(jnp.int32, (128, RANK), 1)
        sel[pl.ds(base, 128), :] = jnp.where(hit, 1.0, 0.0).astype(BF16)
        return carry

    lax.fori_loop(0, 8, choose, 0)

    piece_of = (lax.broadcasted_iota(jnp.int32, (ROWS, RANK), 1) // 4) % 4
    total = jnp.zeros((ROWS, RANK), F32)
    for g in range(4):
        acc = jnp.zeros((ROWS, RANK), F32)
        for j in range(PARTS):
            got = lax.dot_general(
                bbuf[:, j * PC:(j + 1) * PC], vbuf[g * 256:(g + 1) * 256, :],
                (((1,), (1,)), ((), ())), preferred_element_type=F32,
            )
            acc = jnp.where(piece_of == j, got, acc)
        a1 = acc.astype(BF16)
        rest = acc - a1.astype(F32)
        a2 = rest.astype(BF16)
        a3 = (rest - a2.astype(F32)).astype(BF16)
        pick = sel[g * 256:(g + 1) * 256, :]
        for a in (a3, a2, a1):
            total = total + jnp.dot(a, pick, preferred_element_type=F32)
    part[...] = total

    tp_id = lambda p: (f, p)
    y_id = lambda p: (p * NZ + z, t)
    z_id = lambda p: (y * NZ + p, t)

    slab = lambda p: pl.ds(pl.multiple_of(p * 16, 16), 16)
    c1 = exchange(lambda p: part.at[slab(p)], lambda p: tbuf.at[p], tp_id, t, ps, pr)
    tbuf[t] = part[slab(t), :]
    arrived(lambda p: tbuf.at[p], tp_id, t, ps, pr)
    sums = tbuf[0]
    for p in range(1, 8):
        sums = sums + tbuf[p]
    proj_ref[slab(t), :] = sums
    c2 = exchange(lambda p: proj_ref.at[slab(t)], lambda p: proj_ref.at[slab(p)], tp_id, t, as_, ar)
    arrived(lambda p: proj_ref.at[slab(p)], tp_id, t, as_, ar)

    pv = proj_ref[...]
    gpart[...] = lax.dot_general(pv, pv, (((0,), (0,)), ((), ())), precision=HIGHEST, preferred_element_type=F32)
    tile = lambda p: (
        pl.ds(pl.multiple_of(t * 32 + (p // 2) * 8, 8), 8),
        pl.ds(pl.multiple_of(lax.rem(p, 2) * 128, 128), 128),
    )
    c3 = exchange(lambda p: gpart.at[tile(p)], lambda p: ybuf.at[p], y_id, y, ys, yr)
    ybuf[y] = gpart[tile(y)]
    arrived(lambda p: ybuf.at[p], y_id, y, ys, yr)
    sums = ybuf[0]
    for p in range(1, 8):
        sums = sums + ybuf[p]
    zbuf[z] = sums
    c4 = exchange(lambda p: zbuf.at[z], lambda p: zbuf.at[p], z_id, z, zs, zr)
    arrived(lambda p: zbuf.at[p], z_id, z, zs, zr)
    sums = zbuf[0]
    for p in range(1, 8):
        sums = sums + zbuf[p]
    gram_ref[tile(y)] = sums
    c5 = exchange(lambda p: gram_ref.at[tile(y)], lambda p: gram_ref.at[tile(p)], y_id, y, bs, br)
    arrived(lambda p: gram_ref.at[tile(p)], y_id, y, bs, br)
    block = lambda p: pl.ds(pl.multiple_of(p * 32, 32), 32)
    c6 = exchange(lambda p: gram_ref.at[block(t)], lambda p: gram_ref.at[block(p)], tp_id, t, ts, tr)
    arrived(lambda p: gram_ref.at[block(p)], tp_id, t, ts, tr)
    finish()
    for copies in (c1, c2, c3, c4, c5, c6):
        for copy in copies:
            copy.wait_send()


def invert_kernel(gram_ref, x_ref, err_ref, sx):
    i = lax.broadcasted_iota(jnp.int32, (RANK, RANK), 0)
    j = lax.broadcasted_iota(jnp.int32, (RANK, RANK), 1)
    diagonal = i == j
    gram = gram_ref[...]
    on = jnp.where(diagonal, gram, 0.0)
    down = lax.rsqrt(jnp.sum(on, axis=1, keepdims=True))
    across = lax.rsqrt(jnp.sum(on, axis=0, keepdims=True))
    sx[:, :RANK] = gram * down * across
    sx[:, RANK:] = jnp.where(diagonal, down, 0.0)

    def miss():
        return jnp.max(jnp.abs(sx[:, :RANK] - jnp.where(diagonal, 1.0, 0.0)))

    def more(state):
        count, err = state
        return jnp.logical_and(count < 16, err > 1e-5)

    def step(state):
        count, _ = state
        e = sx[:, :RANK] - jnp.where(diagonal, 1.0, 0.0)
        w = jnp.where(i > j, -e, jnp.where(diagonal, 1.0 - 0.5 * e, 0.0))
        out = jnp.dot(w, sx[...], precision=HIGHEST, preferred_element_type=F32)
        sx[:, RANK:] = out[:, RANK:]
        sx[:, :RANK] = lax.dot_general(
            out[:, :RANK], w, (((1,), (1,)), ((), ())), precision=HIGHEST, preferred_element_type=F32
        )
        return count + 1, miss()

    _, err = lax.while_loop(more, step, (jnp.int32(0), miss()))
    x_ref[...] = sx[:, RANK:]
    err_ref[0] = err


def back_kernel(
    m_ref, g_ref, proj_ref, x_ref, mom_ref, own_ref, upd_ref,
    mbuf, gbuf, bbuf, wbuf, obuf, land, ring, near, far, sqbuf,
    local_sem, s1, r1, s2, r2, s3, r3, s4, r4, qs, qr,
):
    f, t, y, z, even = place()
    me = own_slot(even, y, z)
    cm = pltpu.make_async_copy(m_ref, mbuf, local_sem.at[0])
    cg = pltpu.make_async_copy(g_ref, gbuf, local_sem.at[1])
    cm.start()
    cg.start()
    ortho = lax.dot_general(
        proj_ref[...], x_ref[...], (((1,), (1,)), ((), ())), precision=HIGHEST, preferred_element_type=F32
    )
    low = ortho.astype(BF16)
    cm.wait()
    cg.wait()
    for j in range(PARTS):
        cols = slice(j * PC, (j + 1) * PC)
        b = (mbuf[:, cols].astype(F32) + gbuf[:, cols].astype(F32)).astype(BF16)
        bbuf[:, cols] = b
        wbuf[j * RANK:(j + 1) * RANK, :] = lax.dot_general(
            low, b, (((0,), (0,)), ((), ())), preferred_element_type=F32
        ).astype(BF16)
    greet(f, t, y, z)

    def hop(ax, d, c, h, src):
        step = 1 if d == 0 else -1
        to = (y * NZ + mod8(z + step)) if ax == 0 else (mod8(y + step) * NZ + z)
        return pltpu.make_async_remote_copy(
            src_ref=src,
            dst_ref=land.at[ax, d, c, h],
            send_sem=s3.at[ax, d, c, h],
            recv_sem=r3.at[ax, d, c, h],
            device_id=(to, t),
            device_id_type=MESH,
        )

    sent = []
    for ax, d, c in STREAMS:
        step = 1 if d == 0 else -1
        pos = z if ax == 0 else y
        n = hops_of(d, c)
        copy = hop(ax, d, c, 0, wbuf.at[chunk(ax, mod8(pos + step * n), c)])
        copy.start()
        sent.append(copy)
    for h in range(4):
        for ax, d, c in STREAMS:
            step = 1 if d == 0 else -1
            pos = z if ax == 0 else y
            n = hops_of(d, c)
            if h < n:
                hop(ax, d, c, h, land.at[ax, d, c, h]).wait_recv()
                if h + 1 < n:
                    mine = wbuf[chunk(ax, mod8(pos + step * (n - h - 1)), c), :]
                    ring[ax, d, c, h] = (mine.astype(F32) + land[ax, d, c, h].astype(F32)).astype(BF16)
                    copy = hop(ax, d, c, h + 1, ring.at[ax, d, c, h])
                    copy.start()
                    sent.append(copy)

    spot = jnp.where(even, y, z)
    for ax in range(2):
        pos = z if ax == 0 else y
        cross = y if ax == 0 else z
        for c in range(2):
            both = wbuf[chunk(ax, pos, c), :].astype(F32)
            for d in range(2):
                both = both + land[ax, d, c, hops_of(d, c) - 1].astype(F32)
            near[ax, c] = both.astype(BF16)
            for i in range(2):
                odd = lax.rem(pos, 2) if ax == 0 else 1 - lax.rem(pos, 2)
                to = 2 * (2 * c + i) + odd

                @pl.when(to != cross)
                def _():
                    pltpu.make_async_remote_copy(
                        src_ref=near.at[ax, c, pl.ds(i * SLOT, SLOT)],
                        dst_ref=far.at[cross],
                        send_sem=s4.at[ax, 2 * c + i],
                        recv_sem=r4.at[cross],
                        device_id=((to * NZ + z) if ax == 0 else (y * NZ + to), t),
                        device_id_type=MESH,
                    ).start()

                @pl.when(to == cross)
                def _():
                    far[cross] = near[ax, c, i * SLOT:(i + 1) * SLOT, :]

    for k in range(1, 8):
        p = mod8(spot + k)
        pltpu.make_async_remote_copy(
            src_ref=far.at[p],
            dst_ref=far.at[p],
            send_sem=s4.at[0, 0],
            recv_sem=r4.at[p],
            device_id=(f, mod8(t + 1)),
            device_id_type=MESH,
        ).wait_recv()
    sums = far[0].astype(F32)
    for p in range(1, 8):
        sums = sums + far[p].astype(F32)
    obuf[rows_of(me), :] = sums.astype(BF16)

    finish = gather(obuf, f, t, y, z, even, s1, r1, s2, r2)

    ones = jnp.ones((8, PC), BF16)
    sq = jnp.zeros((8, RANK), F32)
    for j in range(PARTS):
        v = obuf[j * RANK:(j + 1) * RANK, :].astype(F32)
        v = v * v
        hi = v.astype(BF16)
        lo = (v - hi.astype(F32)).astype(BF16)
        for a in (lo, hi):
            sq = sq + lax.dot_general(ones, a, (((1,), (1,)), ((), ())), preferred_element_type=F32)
    tp_id = lambda p: (f, p)
    sqbuf[t] = sq
    c1 = exchange(lambda p: sqbuf.at[t], lambda p: sqbuf.at[p], tp_id, t, qs, qr)
    arrived(lambda p: sqbuf.at[p], tp_id, t, qs, qr)
    squares = sqbuf[0]
    for p in range(1, 8):
        squares = squares + sqbuf[p]
    squares = squares + epsilon
    scale = jnp.sqrt(squares)[0:1, :].astype(BF16).astype(F32)
    inverse = jnp.transpose(jnp.broadcast_to(lax.rsqrt(squares)[0:1, :], (128, RANK)))[:, 0:1]
    scaled = (low.astype(F32) * scale).astype(BF16)
    pick = jnp.where(
        lax.broadcasted_iota(jnp.int32, (8, RANK), 0) + f * OWN == lax.broadcasted_iota(jnp.int32, (8, RANK), 1),
        1.0, 0.0,
    ).astype(BF16)
    for j in range(PARTS):
        cols = slice(j * PC, (j + 1) * PC)
        nb = (obuf[j * RANK:(j + 1) * RANK, :].astype(F32) * inverse).astype(BF16)
        own_ref[:, cols] = jnp.dot(pick, nb, preferred_element_type=F32)[0:OWN].astype(BF16)
        upd_ref[:, cols] = (UNIT * jnp.dot(low, nb, preferred_element_type=F32)).astype(BF16)
        mom_ref[:, cols] = (
            bbuf[:, cols].astype(F32) - (1.0 - momentum_decay) * jnp.dot(scaled, nb, preferred_element_type=F32)
        ).astype(BF16)

    finish()
    for copy in sent:
        copy.wait_send()
    for copy in c1:
        copy.wait_send()
    for ax in range(2):
        pos = z if ax == 0 else y
        cross = y if ax == 0 else z
        for c in range(2):
            for i in range(2):
                odd = lax.rem(pos, 2) if ax == 0 else 1 - lax.rem(pos, 2)
                to = 2 * (2 * c + i) + odd

                @pl.when(to != cross)
                def _():
                    pltpu.make_async_remote_copy(
                        src_ref=near.at[ax, c, pl.ds(i * SLOT, SLOT)],
                        dst_ref=far.at[cross],
                        send_sem=s4.at[ax, 2 * c + i],
                        recv_sem=r4.at[cross],
                        device_id=(f, mod8(t + 1)),
                        device_id_type=MESH,
                    ).wait_send()


VMEM = pl.BlockSpec(memory_space=pltpu.VMEM)
ANY = pl.BlockSpec(memory_space=pl.ANY)
DMA = pltpu.SemaphoreType.DMA
LIMIT = 48 * 2**20


def project(momentum, gradient, basis_rows):
    return pl.pallas_call(
        project_kernel,
        out_shape=[jax.ShapeDtypeStruct((ROWS, RANK), F32), jax.ShapeDtypeStruct((RANK, RANK), F32)],
        in_specs=[ANY, ANY, ANY],
        out_specs=[VMEM, VMEM],
        scratch_shapes=[
            pltpu.VMEM((NF * SLOT, PC), BF16),
            pltpu.VMEM((ROWS, COLS), BF16),
            pltpu.VMEM((ROWS, COLS), BF16),
            pltpu.VMEM((ROWS, COLS), BF16),
            pltpu.VMEM((OWN, COLS), BF16),
            pltpu.VMEM((NF * SLOT, RANK), BF16),
            pltpu.VMEM((ROWS, RANK), F32),
            pltpu.VMEM((8, 16, RANK), F32),
            pltpu.VMEM((RANK, RANK), F32),
            pltpu.VMEM((8, 8, 128), F32),
            pltpu.VMEM((8, 8, 128), F32),
            DMA((3,)),
            DMA((8,)), DMA((8,)), DMA((2, 2, 2, 4)), DMA((2, 2, 2, 4)),
        ] + [DMA((8,))] * 12,
        compiler_params=pltpu.CompilerParams(collective_id=0, has_side_effects=True, vmem_limit_bytes=LIMIT),
        name="project",
    )(momentum, gradient, basis_rows)


def invert(gram):
    return pl.pallas_call(
        invert_kernel,
        out_shape=[jax.ShapeDtypeStruct((RANK, RANK), F32), jax.ShapeDtypeStruct((1,), F32)],
        in_specs=[VMEM],
        out_specs=[VMEM, pl.BlockSpec(memory_space=pltpu.SMEM)],
        scratch_shapes=[pltpu.VMEM((RANK, 2 * RANK), F32)],
        compiler_params=pltpu.CompilerParams(vmem_limit_bytes=LIMIT),
        name="invert",
    )(gram)


def back(momentum, gradient, proj, x):
    return pl.pallas_call(
        back_kernel,
        out_shape=[
            jax.ShapeDtypeStruct((ROWS, COLS), BF16),
            jax.ShapeDtypeStruct((OWN, COLS), BF16),
            jax.ShapeDtypeStruct((ROWS, COLS), BF16),
        ],
        in_specs=[ANY, ANY, VMEM, VMEM],
        out_specs=[VMEM, VMEM, VMEM],
        scratch_shapes=[
            pltpu.VMEM((ROWS, COLS), BF16),
            pltpu.VMEM((ROWS, COLS), BF16),
            pltpu.VMEM((ROWS, COLS), BF16),
            pltpu.VMEM((NF * SLOT, PC), BF16),
            pltpu.VMEM((NF * SLOT, PC), BF16),
            pltpu.VMEM((2, 2, 2, 4, 2 * SLOT, PC), BF16),
            pltpu.VMEM((2, 2, 2, 3, 2 * SLOT, PC), BF16),
            pltpu.VMEM((2, 2, 2 * SLOT, PC), BF16),
            pltpu.VMEM((8, SLOT, PC), BF16),
            pltpu.VMEM((8, 8, RANK), F32),
            DMA((2,)),
            DMA((8,)), DMA((8,)), DMA((2, 2, 2, 4)), DMA((2, 2, 2, 4)),
            DMA((2, 2, 2, 4)), DMA((2, 2, 2, 4)), DMA((2, 4)), DMA((8,)), DMA((8,)), DMA((8,)),
        ],
        compiler_params=pltpu.CompilerParams(collective_id=1, has_side_effects=True, vmem_limit_bytes=LIMIT),
        name="back",
    )(momentum, gradient, proj, x)


def direct(gram):
    lower_factor = jnp.linalg.cholesky(gram)
    return lax.linalg.triangular_solve(lower_factor, jnp.eye(RANK, dtype=F32), left_side=True, lower=True)


def local(momentum, gradient, basis_rows):
    proj, gram = project(momentum, gradient, basis_rows)
    x, err = invert(gram)
    x = lax.cond(err[0] < 1e-5, lambda g, v: v, lambda g, v: direct(g), gram, x)
    return tuple(back(momentum, gradient, proj, x))


def solution(mesh):
    return jax.shard_map(
        local,
        mesh=mesh,
        in_specs=(P("fsdp", "tp"), P("fsdp", "tp"), P("fsdp", "tp")),
        out_specs=(P("fsdp", "tp"), P("fsdp", "tp"), P("fsdp", "tp")),
        check_vma=False,
    )
```

time: 587 us -> 202 us (0.34)
  waiting for transfers between devices: 474 us -> 0 us
  Pallas kernels: 0 us -> 134 us
  blocking collectives: 16.4 us -> 0 us
  between operations: 15.2 us -> 1.35 us
  matrix products: 11.7 us -> 1.31 us
    psum x3 -> x0, waiting for transfers between devices: 386 us -> none  [the longest x1 165 us: local(): back_factor = lax.psum(partial_back, 'fsdp')]
    pallas_call x0 -> x3, Pallas kernels: none -> 134 us  [the longest x1 69.5 us: project(): pl.pallas_call(project_kernel, out_shape=[jax.ShapeDtypeStruct((ROWS, RAN...]
    all_gather x1 -> x0, waiting for transfers between devices: 87.7 us -> none  [local(): lax.all_gather(basis_rows, 'fsdp', axis=0, tiled=True)]
    psum x1 -> x0, blocking collectives: 16.4 us -> none  [local(): column_squares = lax.psum(jnp.sum(back_factor * back_factor, axis=1), 'tp')]
    dot_general x5 -> x0, matrix products: 10.4 us -> none  [the longest x1 2.89 us: local(): lax.dot_general(buffer, lax.all_gather(basis_rows, 'fsdp', axis=0, tiled=...]
    another operation x9 -> x10, other arithmetic: 53.7 us -> 53.7 us  [the longest x6 34 us: direct(): lower_factor = jnp.linalg.cholesky(gram)]
  transfers between devices with their start and end apart: 4 -> 0, of which waited for: 4 -> 0; matrix products, arithmetic and copies ran while one was open for 0% -> 0% of each run, Pallas kernels for 0% -> 0%
where the time goes in v1:
time: 202 us
  Pallas kernels  134 us (66%)
  other arithmetic  53.8 us (27%)
  local copies, waits for them, and re-layouts  9.69 us (5%)
  loops' own time  2.12 us (1%)
    pallas_call x1, Pallas kernels, project(): pl.pallas_call(project_kernel, out_shape=[jax.ShapeDtypeStruct((ROWS, RAN...  69.5 us
    pallas_call x1, Pallas kernels, back(): pl.pallas_call(back_kernel, out_shape=[jax.ShapeDtypeStruct((ROWS, COLS),...  59.5 us
    another operation x6, other arithmetic, direct(): lower_factor = jnp.linalg.cholesky(gram)  34 us
    another operation x4, other arithmetic, direct(): lax.linalg.triangular_solve(lower_factor, jnp.eye(RANK, dtype=F32), left_...  19.7 us
    unnamed x13, local copies, waits for them, and re-layouts  5.57 us
    pallas_call x1, Pallas kernels, invert(): pl.pallas_call(invert_kernel, out_shape=[jax.ShapeDtypeStruct((RANK, RANK...  4.72 us

profile of v1, /device:TPU:1, one launch (start us, length us, event | category | flops | bytes accessed | tf_op | source)
XLA Modules:
  0.0 202.0 jit_solution(4758565227442875292)
XLA Ops:
  0.6 0.0 copy-start
  0.6 1.2 copy-done
  1.8 1.2 copy-done.2
  3.0 0.7 copy-done.4
  3.7 69.5 %project.1 = (f32[128,256]{1,0:T(8,128)S(1)}, f32[256,256]{1,0:T(8,128)S(1)}) custom-call(bf16[128,3584]{1,0:T(8,128)(2,1)S(1)} %copy-done, bf16[128,3584]{1,0:T(8,128)(2,1)S(1)} %copy-done.2, bf16[4,3584]{1,0:T(4,128)(2,1)S(1)} %copy-done.4), custom_call_target="tpu_custom_call" | custom-call | tf_op jit(solution)/shard_map/project/pallas_call | solution.py:510
  73.3 4.7 %invert.1 = (f32[256,256]{1,0:T(8,128)S(1)}, f32[1]{0:T(128)}) custom-call(f32[256,256]{1,0:T(8,128)S(1)} %get-tuple-element.13.gram_ref), custom_call_target="tpu_custom_call" | custom-call | tf_op jit(solution)/shard_map/invert/pallas_call | solution.py:536
  78.6 0.0 copy-start.1
  78.7 0.0 copy-start.3
  78.7 61.3 %conditional.1 = (f32[256,256]{1,0:T(8,128)S(1)}) conditional(s32[]{:T(128)} %bitcast.5, (f32[256,256]{1,0:T(8,128)S(1)}) %tuple.16, f32[256,256]{1,0:T(8,128)S(1)} %get-tuple-element.15), branch_computations={%region_0.5_spmd, %region_5.6_spmd} | conditional | flops 202064128 | bytes 4720855 | solution.py:585
  78.9 0.1 triangular_solve.11
  79.0 0.1 copy.8
  79.2 11.7 %cholesky.5 = f32[128,128]{1,0:T(8,128)S(1)} custom-call(f32[128,128]{1,0:T(8,128)S(1)} %cholesky.46), custom_call_target="Cholesky" | custom-call | tf_op jit(solution)/shard_map/cond/branch_0_fun/jit(cholesky)/cholesky | solution.py:578
  90.9 9.8 %custom-call.12 = f32[1,128,128]{1,2,0:T(8,128)S(1)} custom-call(f32[1,128,128]{2,1,0:T(8,128)S(1)} %get-tuple-element.38), custom_call_target="InvertDiagBlocksLowerTriangular" | custom-call | tf_op jit(solution)/shard_map/cond/branch_0_fun/jit(cholesky)/cholesky | solution.py:578
  100.8 0.2 constant_dynamic-update-slice_fusion.1
  101.0 0.3 convolution_subtract_fusion.1
  101.2 11.7 %cholesky.29 = f32[128,128]{1,0:T(8,128)S(1)} custom-call(f32[128,128]{1,0:T(8,128)S(1)} %convolution_subtract_fusion.1), custom_call_target="Cholesky" | custom-call | tf_op jit(solution)/shard_map/cond/branch_0_fun/jit(cholesky)/cholesky | solution.py:578
  113.0 0.7 compare_reduce_fusion
  115.0 4.2 %while.1 = (s32[]{:T(128)}, f32[256,256]{1,0:T(8,128)S(1)}, s32[2,2]{1,0:T(2,128)S(1)}, f32[2,128,128]{2,1,0:T(8,128)S(1)}, s32[]{:T(128)}) while((s32[]{:T(128)}, f32[256,256]{1,0:T(8,128)S(1)}, s32[2,2]{1,0:T(2,128)S(1)}, f32[2,128,128]{2,1,0:T(8,128)S(1)}, s32[]{:T(128)}) %tuple.32), condition=%wide.while_cond, body=%wide.while_body.sunk | while | flops 2 | bytes 131189 | solution.py:579
  115.2 0.6 fusion.14
  115.8 1.4 bitcast_dynamic-update-slice_fusion.2
  117.2 0.6 fusion.14
  117.8 1.4 bitcast_dynamic-update-slice_fusion.2
  119.1 19.7 %custom-call.13 = f32[2,128,128]{1,2,0:T(8,128)S(1)} custom-call(f32[2,128,128]{2,1,0:T(8,128)S(1)} %get-tuple-element.23), custom_call_target="InvertDiagBlocksLowerTriangular" | custom-call | tf_op jit(solution)/shard_map/cond/branch_0_fun/triangular_solve | solution.py:579
  138.8 0.3 fusion.1
  139.1 0.3 convolution_subtract_fusion
  139.4 0.3 fusion.4
  140.0 0.0 copy-done.1
  140.0 0.0 copy-done.3
  140.0 59.5 %back.1 = (bf16[128,3584]{1,0:T(8,128)(2,1)S(1)}, bf16[4,3584]{1,0:T(4,128)(2,1)S(1)}, bf16[128,3584]{1,0:T(8,128)(2,1)S(1)}) custom-call(bf16[128,3584]{1,0:T(8,128)(2,1)S(1)} %copy-done.1, bf16[128,3584]{1,0:T(8,128)(2,1)S(1)} %copy-done.3, f32[128,256]{1,0:T(8,128)S(1)} %get-tuple-element.12.proj_ref, f32[256,256]{1,0:T(8,128)S(1)} %get-tuple-element.93.x_ref), custom_call_target="tpu_custom_call" | custom-call | tf_op jit(solution)/shard_map/back/pallas_call | solution.py:548
  199.6 0.9 copy.26
  200.5 0.6 copy.27
  201.1 0.9 copy.28
  (14 shorter events, 0.2 us)
Async XLA Ops:
  0.6 1.2 copy-start
  1.8 1.2 copy-start.2
  3.0 0.7 copy-start.4
  78.6 61.3 %copy-start.1 = (bf16[128,3584]{1,0:T(8,128)(2,1)S(1)}, bf16[128,3584]{1,0:T(8,128)(2,1)}, u32[]{:S(2)}) copy-start(bf16[128,3584]{1,0:T(8,128)(2,1)} %m_ref.3) | copy-start | bytes 2752516
  78.7 61.3 %copy-start.3 = (bf16[128,3584]{1,0:T(8,128)(2,1)S(1)}, bf16[128,3584]{1,0:T(8,128)(2,1)}, u32[]{:S(2)}) copy-start(bf16[128,3584]{1,0:T(8,128)(2,1)} %g_ref.3) | copy-start | bytes 2752516

commit v2 on v0

v2 whole, which is shorter than its diff:
```python
import functools
import math

import jax
import jax.numpy as jnp
from jax import lax
from jax.experimental import pallas as pl
from jax.experimental.pallas import tpu as pltpu
from jax.sharding import PartitionSpec as P

D = 8192
FF = 28672
RANK = 256
NY = 8
NZ = 8
NF = 64
NT = 8
ROWS = D // NF
COLS = FF // NT
OWN = RANK // NF
PARTS = 4
PC = COLS // PARTS
SLOT = 16
CUT = COLS // NF
PAD = 64

epsilon = 1e-06
momentum_decay = 0.95
UNIT = math.sqrt(D * FF / RANK)

F32 = jnp.float32
BF16 = jnp.bfloat16
MESH = pl.DeviceIdType.MESH
HIGHEST = lax.Precision.HIGHEST


def mod8(v):
    return lax.rem(v + 16, 8)


def place():
    f = lax.axis_index("fsdp")
    t = lax.axis_index("tp")
    y = f // NZ
    z = lax.rem(f, NZ)
    even = lax.rem(y + z, 2) == 0
    return f, t, y, z, even


def line(even, y, z, k):
    along_y = jnp.where(even, k, 0)
    along_z = jnp.where(even, 0, k)
    return mod8(y + along_y) * NZ + mod8(z + along_z)


def own_slot(even, y, z):
    return jnp.where(even, z * 4 + y // 2, 32 + y * 4 + z // 2)


def greet(f, t, y, z):
    barrier = pltpu.get_barrier_semaphore()
    for k in range(1, 8):
        pl.semaphore_signal(barrier, inc=1, device_id=(mod8(y + k) * NZ + z, t), device_id_type=MESH)
        pl.semaphore_signal(barrier, inc=1, device_id=(y * NZ + mod8(z + k), t), device_id_type=MESH)
        pl.semaphore_signal(barrier, inc=1, device_id=(f, mod8(t + k)), device_id_type=MESH)
    pl.semaphore_wait(barrier, 21)


ORDER = (0, 1, 3, 2)


def fourth(d, i):
    return (i < 2) if d == 0 else (i >= 2)


def slot_of(ax, origin, i):
    return ax * 32 + origin * 4 + i


def beside(ax, d, y, z):
    step = 1 if d == 0 else -1
    return (y * NZ + mod8(z + step)) if ax == 0 else (mod8(y + step) * NZ + z)


def gather(buf, size, f, t, y, z, even, s1, r1, s2, r2, between):
    rows = lambda slot: buf.at[pl.ds(pl.multiple_of(slot * size, size), size)]
    me = own_slot(even, y, z)
    at = (z, y)
    half = (y // 2, z // 2)
    home = (even, jnp.logical_not(even))
    here = jnp.where(even, y // 2, 4 + z // 2)
    aside = (f, mod8(t + 1))

    def straight(k, to):
        return pltpu.make_async_remote_copy(
            src_ref=rows(me), dst_ref=rows(me), send_sem=s1.at[k], recv_sem=r1.at[here],
            device_id=to, device_id_type=MESH,
        )

    def copy(ax, d, i, h, origin, to):
        slot = slot_of(ax, origin, i)
        return pltpu.make_async_remote_copy(
            src_ref=rows(slot), dst_ref=rows(slot), send_sem=s2.at[ax, d, i, h], recv_sem=r2.at[ax, d, i, h],
            device_id=to, device_id_type=MESH,
        )

    def send(ax, d, i, h):
        step = 1 if d == 0 else -1
        copy(ax, d, i, h, mod8(at[ax] - step * h), (beside(ax, d, y, z), t)).start()

    def landed(ax, d, i, h):
        step = 1 if d == 0 else -1
        copy(ax, d, i, h, mod8(at[ax] - step * (h + 1)), aside).wait_recv()

    for ax in range(2):
        @pl.when(home[ax])
        def _():
            for d in range(2):
                send(ax, d, half[ax], 0)
    for k in (1, 7, 2, 6, 3, 5, 4):
        straight(k, (line(even, y, z, k), t)).start()
    between[0]()
    for r in ORDER:
        for ax in range(2):
            i = lax.rem(half[ax] + r, 4)

            def first():
                slot = slot_of(ax, at[ax], i)
                pltpu.make_async_remote_copy(
                    src_ref=rows(slot), dst_ref=rows(slot), send_sem=s1.at[0], recv_sem=r1.at[ax * 4 + i],
                    device_id=aside, device_id_type=MESH,
                ).wait_recv()
                for d in range(2):
                    send(ax, d, i, 0)

            if r == 0:
                pl.when(jnp.logical_not(home[ax]))(first)
            else:
                first()
    between[1]()
    for h in range(4):
        for r in ORDER:
            for ax in range(2):
                i = lax.rem(half[ax] + r, 4)
                for d in range(2):
                    if h < 2:
                        landed(ax, d, i, h)
                        send(ax, d, i, h + 1)
                    elif h == 2:
                        landed(ax, d, i, h)

                        @pl.when(fourth(d, i))
                        def _():
                            send(ax, d, i, 3)
                    else:

                        @pl.when(fourth(d, i))
                        def _():
                            landed(ax, d, i, 3)
        between[h + 2]()

    def finish():
        for k in range(1, 8):
            straight(k, aside).wait_send()
        for ax in range(2):
            for d in range(2):
                for i in range(4):
                    for h in range(4 if fourth(d, i) else 3):
                        copy(ax, d, i, h, at[ax], aside).wait_send()

    return finish


def exchange(src_of, dst_of, ids, pos, send, recv):
    copies = []
    for k in (4, 3, 5, 2, 6, 1, 7):
        p = mod8(pos + k)
        copy = pltpu.make_async_remote_copy(
            src_ref=src_of(p),
            dst_ref=dst_of(pos),
            send_sem=send.at[k],
            recv_sem=recv.at[8 - k],
            device_id=ids(p),
            device_id_type=MESH,
        )
        copy.start()
        copies.append(copy)
    return copies


def arrived(dst_of, ids, pos, send, recv):
    for k in range(1, 8):
        p = mod8(pos + k)
        pltpu.make_async_remote_copy(
            src_ref=dst_of(p),
            dst_ref=dst_of(p),
            send_sem=send.at[k],
            recv_sem=recv.at[k],
            device_id=ids(p),
            device_id_type=MESH,
        ).wait_recv()


def thirds(v):
    a1 = v.astype(BF16)
    rest = v - a1.astype(F32)
    a2 = rest.astype(BF16)
    return a1, a2, (rest - a2.astype(F32)).astype(BF16)


def project_kernel(
    m_ref, g_ref, basis_ref, proj_ref, gram_ref, z_ref,
    vbuf, bbuf, mbuf, gbuf, stage, sel, part, tbuf, gpart, ybuf, zbuf, work, land, near, far,
    local_sem, s1, r1, s2, r2, s3, r3, s4, r4, ps, pr, as_, ar, ys, yr, zs, zr, bs, br, ts, tr,
):
    f, t, y, z, even = place()
    me = own_slot(even, y, z)
    at = (z, y)
    aside = (f, mod8(t + 1))
    cm = pltpu.make_async_copy(m_ref, mbuf, local_sem.at[0])
    cg = pltpu.make_async_copy(g_ref, gbuf, local_sem.at[1])
    cb = pltpu.make_async_copy(basis_ref, stage, local_sem.at[2])
    cb.start()
    cm.start()
    cg.start()
    cb.wait()
    own = stage[...].astype(F32)
    pieces = [own[:, j * PC:(j + 1) * PC] for j in range(PARTS)]
    vbuf[pl.ds(pl.multiple_of(me * SLOT, SLOT), SLOT), :] = jnp.concatenate(pieces, axis=0).astype(BF16)
    greet(f, t, y, z)

    def prepare():
        cm.wait()
        cg.wait()
        for j in range(PARTS):
            cols = slice(j * PC, (j + 1) * PC)
            bbuf[:, cols] = (mbuf[:, cols].astype(F32) + gbuf[:, cols].astype(F32)).astype(BF16)
        part[...] = jnp.zeros((ROWS, RANK), F32)

        def choose(i, carry):
            base = pl.multiple_of(i * 128, 128)
            row = base + lax.broadcasted_iota(jnp.int32, (128, RANK), 0)
            slot = row // SLOT
            first, second = (slot // 4) % 8, slot % 4
            yf = 2 * second + (first % 2)
            zo = 2 * second + (1 - first % 2)
            dev = jnp.where(slot < 32, yf * NZ + first, first * NZ + zo)
            hit = dev * OWN + row % 4 == lax.broadcasted_iota(jnp.int32, (128, RANK), 1)
            sel[pl.ds(base, 128), :] = jnp.where(hit, 1.0, 0.0).astype(BF16)
            return carry

        lax.fori_loop(0, 8, choose, 0)

    def level(h):
        def run():
            if h == 0 or h == 4:
                starts = [slot_of(ax, mod8(at[ax] + h), 0) * SLOT for ax in range(2)]
            else:
                starts = [slot_of(ax, mod8(at[ax] + s), 0) * SLOT for ax in range(2) for s in (h, -h)]
            spans = [pl.ds(pl.multiple_of(s, 64), 64) for s in starts]
            v = jnp.concatenate([vbuf[s, :] for s in spans], axis=0)
            pick = jnp.concatenate([sel[s, :] for s in spans], axis=0)
            piece_of = (lax.broadcasted_iota(jnp.int32, (ROWS, v.shape[0]), 1) // 4) % 4
            acc = jnp.zeros((ROWS, v.shape[0]), F32)
            for j in range(PARTS):
                got = lax.dot_general(
                    bbuf[:, j * PC:(j + 1) * PC], v, (((1,), (1,)), ((), ())), preferred_element_type=F32
                )
                acc = jnp.where(piece_of == j, got, acc)
            total = part[...]
            for a in thirds(acc)[::-1]:
                total = total + jnp.dot(a, pick, preferred_element_type=F32)
            part[...] = total
        return run

    finish = gather(
        vbuf, SLOT, f, t, y, z, even, s1, r1, s2, r2,
        [prepare, level(0), level(1), level(2), level(3), level(4)],
    )

    tp_id = lambda p: (f, p)
    y_id = lambda p: (p * NZ + z, t)
    z_id = lambda p: (y * NZ + p, t)

    slab = lambda p: pl.ds(pl.multiple_of(p * 16, 16), 16)
    c1 = exchange(lambda p: part.at[slab(p)], lambda p: tbuf.at[p], tp_id, t, ps, pr)
    tbuf[t] = part[slab(t), :]
    arrived(lambda p: tbuf.at[p], tp_id, t, ps, pr)
    sums = tbuf[0]
    for p in range(1, 8):
        sums = sums + tbuf[p]
    proj_ref[slab(t), :] = sums
    c2 = exchange(lambda p: proj_ref.at[slab(t)], lambda p: proj_ref.at[slab(p)], tp_id, t, as_, ar)
    arrived(lambda p: proj_ref.at[slab(p)], tp_id, t, as_, ar)

    pv = proj_ref[...]
    gpart[...] = lax.dot_general(pv, pv, (((0,), (0,)), ((), ())), precision=HIGHEST, preferred_element_type=F32)
    tile = lambda p: (
        pl.ds(pl.multiple_of(t * 32 + (p // 2) * 8, 8), 8),
        pl.ds(pl.multiple_of(lax.rem(p, 2) * 128, 128), 128),
    )
    c3 = exchange(lambda p: gpart.at[tile(p)], lambda p: ybuf.at[p], y_id, y, ys, yr)
    ybuf[y] = gpart[tile(y)]

    split = thirds(pv)
    for j in range(7):
        cols = slice(j * 512, (j + 1) * 512)
        total = jnp.zeros((512, RANK), F32)
        for a in split[::-1]:
            total = total + lax.dot_general(
                bbuf[:, cols], a, (((0,), (0,)), ((), ())), preferred_element_type=F32
            )
        work[cols, :] = total
    cut = lambda ax, origin, i: pl.ds(pl.multiple_of(slot_of(ax, origin, i) * CUT, 8), CUT)
    streams = [(ax, d, i) for i in range(4) for ax in range(2) for d in range(2)]
    hops = lambda d, i: 4 if fourth(d, i) else 3
    sent = []

    def pass_on(ax, d, i, h, src):
        copy = pltpu.make_async_remote_copy(
            src_ref=src, dst_ref=land.at[ax, d, i, h], send_sem=s3.at[ax, d, i, h], recv_sem=r3.at[ax, d, i, h],
            device_id=(beside(ax, d, y, z), t), device_id_type=MESH,
        )
        copy.start()
        sent.append(copy)

    def came(ax, d, i, h):
        pltpu.make_async_remote_copy(
            src_ref=land.at[ax, d, i, h], dst_ref=land.at[ax, d, i, h], send_sem=s3.at[ax, d, i, h],
            recv_sem=r3.at[ax, d, i, h], device_id=aside, device_id_type=MESH,
        ).wait_recv()

    def ring(h):
        for ax, d, i in streams:
            n = hops(d, i)
            if h < n:
                came(ax, d, i, h)
                if h + 1 < n:
                    step = 1 if d == 0 else -1
                    land[ax, d, i, h] = land[ax, d, i, h] + work[cut(ax, mod8(at[ax] + step * (n - h - 1)), i), :]
                    pass_on(ax, d, i, h + 1, land.at[ax, d, i, h])

    for ax, d, i in streams:
        step = 1 if d == 0 else -1
        pass_on(ax, d, i, 0, work.at[cut(ax, mod8(at[ax] + step * hops(d, i)), i)])
    arrived(lambda p: ybuf.at[p], y_id, y, ys, yr)
    sums = ybuf[0]
    for p in range(1, 8):
        sums = sums + ybuf[p]
    zbuf[z] = sums
    c4 = exchange(lambda p: zbuf.at[z], lambda p: zbuf.at[p], z_id, z, zs, zr)
    ring(0)
    arrived(lambda p: zbuf.at[p], z_id, z, zs, zr)
    sums = zbuf[0]
    for p in range(1, 8):
        sums = sums + zbuf[p]
    gram_ref[tile(y)] = sums
    c5 = exchange(lambda p: gram_ref.at[tile(y)], lambda p: gram_ref.at[tile(p)], y_id, y, bs, br)
    ring(1)
    arrived(lambda p: gram_ref.at[tile(p)], y_id, y, bs, br)
    block = lambda p: pl.ds(pl.multiple_of(p * 32, 32), 32)
    c6 = exchange(lambda p: gram_ref.at[block(t)], lambda p: gram_ref.at[block(p)], tp_id, t, ts, tr)
    ring(2)
    ring(3)

    spot = jnp.where(even, y, z)

    def target(ax, i):
        odd = lax.rem(at[ax], 2) if ax == 0 else 1 - lax.rem(at[ax], 2)
        return 2 * i + odd

    def cross(ax, i, device):
        return pltpu.make_async_remote_copy(
            src_ref=near.at[ax, i], dst_ref=far.at[at[1 - ax]], send_sem=s4.at[ax, i], recv_sem=r4.at[at[1 - ax]],
            device_id=device, device_id_type=MESH,
        )

    for ax in range(2):
        for i in range(4):
            both = work[cut(ax, at[ax], i), :]
            for d in range(2):
                both = both + land[ax, d, i, hops(d, i) - 1]
            near[ax, i] = both
            to = target(ax, i)

            @pl.when(to != at[1 - ax])
            def _():
                cross(ax, i, ((to * NZ + z) if ax == 0 else (y * NZ + to), t)).start()

            @pl.when(to == at[1 - ax])
            def _():
                far[at[1 - ax]] = both

    arrived(lambda p: gram_ref.at[block(p)], tp_id, t, ts, tr)
    for k in range(1, 8):
        p = mod8(spot + k)
        pltpu.make_async_remote_copy(
            src_ref=far.at[p], dst_ref=far.at[p], send_sem=s4.at[0, 0], recv_sem=r4.at[p],
            device_id=aside, device_id_type=MESH,
        ).wait_recv()
    sums = far[0]
    for p in range(1, 8):
        sums = sums + far[p]
    z_ref[...] = sums
    finish()
    for copies in (c1, c2, c3, c4, c5, c6, sent):
        for copy in copies:
            copy.wait_send()
    for ax in range(2):
        for i in range(4):
            @pl.when(target(ax, i) != at[1 - ax])
            def _():
                cross(ax, i, aside).wait_send()


def invert_kernel(gram_ref, x_ref, err_ref, sx):
    i = lax.broadcasted_iota(jnp.int32, (RANK, RANK), 0)
    j = lax.broadcasted_iota(jnp.int32, (RANK, RANK), 1)
    diagonal = i == j
    gram = gram_ref[...]
    on = jnp.where(diagonal, gram, 0.0)
    down = lax.rsqrt(jnp.sum(on, axis=1, keepdims=True))
    across = lax.rsqrt(jnp.sum(on, axis=0, keepdims=True))
    sx[:, :RANK] = gram * down * across
    sx[:, RANK:] = jnp.where(diagonal, down, 0.0)

    def miss():
        return jnp.max(jnp.abs(sx[:, :RANK] - jnp.where(diagonal, 1.0, 0.0)))

    def more(state):
        count, err = state
        return jnp.logical_and(count < 16, err > 1e-5)

    def step(state):
        count, _ = state
        e = sx[:, :RANK] - jnp.where(diagonal, 1.0, 0.0)
        w = jnp.where(i > j, -e, jnp.where(diagonal, 1.0 - 0.5 * e, 0.0))
        out = jnp.dot(w, sx[...], precision=HIGHEST, preferred_element_type=F32)
        sx[:, RANK:] = out[:, RANK:]
        sx[:, :RANK] = lax.dot_general(
            out[:, :RANK], w, (((1,), (1,)), ((), ())), precision=HIGHEST, preferred_element_type=F32
        )
        return count + 1, miss()

    _, err = lax.while_loop(more, step, (jnp.int32(0), miss()))
    x_ref[...] = sx[:, RANK:]
    err_ref[0] = err


def back_kernel(
    m_ref, g_ref, proj_ref, x_ref, z_ref, mom_ref, own_ref, upd_ref,
    mbuf, gbuf, bbuf, obuf, qbuf, tbuf, ybuf, zbuf,
    local_sem, s1, r1, s2, r2, ts, tr, ys, yr, zs, zr,
):
    f, t, y, z, even = place()
    me = own_slot(even, y, z)
    cm = pltpu.make_async_copy(m_ref, mbuf, local_sem.at[0])
    cg = pltpu.make_async_copy(g_ref, gbuf, local_sem.at[1])
    cm.start()
    cg.start()
    tp_id = lambda p: (f, p)
    y_id = lambda p: (p * NZ + z, t)
    z_id = lambda p: (y * NZ + p, t)
    mine = lax.dot_general(
        z_ref[...], x_ref[...], (((1,), (1,)), ((), ())), precision=HIGHEST, preferred_element_type=F32
    )
    obuf[pl.ds(pl.multiple_of(me * PAD, PAD), PAD), :] = jnp.concatenate(
        [mine, jnp.zeros((PAD - CUT, RANK), F32)], axis=0
    ).astype(BF16)
    tbuf[t] = jnp.broadcast_to(jnp.sum(mine * mine, axis=0, keepdims=True), (8, RANK))
    greet(f, t, y, z)
    waits = []

    def open_squares():
        waits.extend(exchange(lambda p: tbuf.at[t], lambda p: tbuf.at[p], tp_id, t, ts, tr))
        cm.wait()
        cg.wait()
        for j in range(PARTS):
            cols = slice(j * PC, (j + 1) * PC)
            bbuf[:, cols] = (mbuf[:, cols].astype(F32) + gbuf[:, cols].astype(F32)).astype(BF16)
        qbuf[...] = lax.dot_general(
            proj_ref[...], x_ref[...], (((1,), (1,)), ((), ())), precision=HIGHEST, preferred_element_type=F32
        ).astype(BF16)

    def fold(buf):
        sums = buf[0]
        for p in range(1, 8):
            sums = sums + buf[p]
        return sums

    def over_y():
        arrived(lambda p: tbuf.at[p], tp_id, t, ts, tr)
        ybuf[y] = fold(tbuf)
        waits.extend(exchange(lambda p: ybuf.at[y], lambda p: ybuf.at[p], y_id, y, ys, yr))

    def over_z():
        arrived(lambda p: ybuf.at[p], y_id, y, ys, yr)
        zbuf[z] = fold(ybuf)
        waits.extend(exchange(lambda p: zbuf.at[z], lambda p: zbuf.at[p], z_id, z, zs, zr))

    nothing = lambda: None
    finish = gather(
        obuf, PAD, f, t, y, z, even, s1, r1, s2, r2,
        [open_squares, over_y, over_z, nothing, nothing, nothing],
    )
    arrived(lambda p: zbuf.at[p], z_id, z, zs, zr)
    squares = fold(zbuf)[0:1, :] + epsilon
    inverse = lax.rsqrt(squares)
    low = qbuf[...]
    scaled = (low.astype(F32) * jnp.sqrt(squares).astype(BF16).astype(F32)).astype(BF16)
    pick = jnp.where(
        lax.broadcasted_iota(jnp.int32, (8, RANK), 0) + f * OWN == lax.broadcasted_iota(jnp.int32, (8, RANK), 1),
        1.0, 0.0,
    ).astype(BF16)
    turn = (((1,), (1,)), ((), ()))
    for j in range(PARTS):
        cols = slice(j * PC, (j + 1) * PC)
        pieces = [obuf[s * PAD:s * PAD + CUT, :].astype(F32) for s in range(j * 16, (j + 1) * 16)]
        nb = (jnp.concatenate(pieces, axis=0) * inverse).astype(BF16)
        own_ref[:, cols] = lax.dot_general(pick, nb, turn, preferred_element_type=F32)[0:OWN].astype(BF16)
        upd_ref[:, cols] = (UNIT * lax.dot_general(low, nb, turn, preferred_element_type=F32)).astype(BF16)
        mom_ref[:, cols] = (
            bbuf[:, cols].astype(F32)
            - (1.0 - momentum_decay) * lax.dot_general(scaled, nb, turn, preferred_element_type=F32)
        ).astype(BF16)
    finish()
    for copy in waits:
        copy.wait_send()


VMEM = pl.BlockSpec(memory_space=pltpu.VMEM)
HBM = pl.BlockSpec(memory_space=pltpu.HBM)
DMA = pltpu.SemaphoreType.DMA
LIMIT = 56 * 2**20
WIDE = (2, 2, 4, 4)


def project(momentum, gradient, basis_rows):
    return pl.pallas_call(
        project_kernel,
        out_shape=[
            jax.ShapeDtypeStruct((ROWS, RANK), F32),
            jax.ShapeDtypeStruct((RANK, RANK), F32),
            jax.ShapeDtypeStruct((CUT, RANK), F32),
        ],
        in_specs=[HBM, HBM, HBM],
        out_specs=[VMEM, VMEM, VMEM],
        scratch_shapes=[
            pltpu.VMEM((NF * SLOT, PC), BF16),
            pltpu.VMEM((ROWS, COLS), BF16),
            pltpu.VMEM((ROWS, COLS), BF16),
            pltpu.VMEM((ROWS, COLS), BF16),
            pltpu.VMEM((OWN, COLS), BF16),
            pltpu.VMEM((NF * SLOT, RANK), BF16),
            pltpu.VMEM((ROWS, RANK), F32),
            pltpu.VMEM((8, 16, RANK), F32),
            pltpu.VMEM((RANK, RANK), F32),
            pltpu.VMEM((8, 8, 128), F32),
            pltpu.VMEM((8, 8, 128), F32),
            pltpu.VMEM((COLS, RANK), F32),
            pltpu.VMEM(WIDE + (CUT, RANK), F32),
            pltpu.VMEM((2, 4, CUT, RANK), F32),
            pltpu.VMEM((8, CUT, RANK), F32),
            DMA((3,)),
            DMA((8,)), DMA((8,)), DMA(WIDE), DMA(WIDE), DMA(WIDE), DMA(WIDE), DMA((2, 4)), DMA((8,)),
        ] + [DMA((8,))] * 12,
        compiler_params=pltpu.CompilerParams(collective_id=0, has_side_effects=True, vmem_limit_bytes=LIMIT),
        name="project",
    )(momentum, gradient, basis_rows)


def invert(gram):
    return pl.pallas_call(
        invert_kernel,
        out_shape=[jax.ShapeDtypeStruct((RANK, RANK), F32), jax.ShapeDtypeStruct((1,), F32)],
        in_specs=[VMEM],
        out_specs=[VMEM, pl.BlockSpec(memory_space=pltpu.SMEM)],
        scratch_shapes=[pltpu.VMEM((RANK, 2 * RANK), F32)],
        compiler_params=pltpu.CompilerParams(vmem_limit_bytes=LIMIT),
        name="invert",
    )(gram)


def back(momentum, gradient, proj, x, zown):
    return pl.pallas_call(
        back_kernel,
        out_shape=[
            jax.ShapeDtypeStruct((ROWS, COLS), BF16),
            jax.ShapeDtypeStruct((OWN, COLS), BF16),
            jax.ShapeDtypeStruct((ROWS, COLS), BF16),
        ],
        in_specs=[HBM, HBM, VMEM, VMEM, VMEM],
        out_specs=[VMEM, VMEM, VMEM],
        scratch_shapes=[
            pltpu.VMEM((ROWS, COLS), BF16),
            pltpu.VMEM((ROWS, COLS), BF16),
            pltpu.VMEM((ROWS, COLS), BF16),
            pltpu.VMEM((NF * PAD, RANK), BF16),
            pltpu.VMEM((ROWS, RANK), BF16),
            pltpu.VMEM((8, 8, RANK), F32),
            pltpu.VMEM((8, 8, RANK), F32),
            pltpu.VMEM((8, 8, RANK), F32),
            DMA((2,)),
            DMA((8,)), DMA((8,)), DMA(WIDE), DMA(WIDE),
        ] + [DMA((8,))] * 6,
        compiler_params=pltpu.CompilerParams(collective_id=1, has_side_effects=True, vmem_limit_bytes=LIMIT),
        name="back",
    )(momentum, gradient, proj, x, zown)


def direct(gram):
    lower_factor = jnp.linalg.cholesky(gram)
    return lax.linalg.triangular_solve(lower_factor, jnp.eye(RANK, dtype=F32), left_side=True, lower=True)


def local(momentum, gradient, basis_rows):
    proj, gram, zown = project(momentum, gradient, basis_rows)
    x, err = invert(gram)
    x = lax.cond(err[0] < 1e-5, lambda g, v: v, lambda g, v: direct(g), gram, x)
    return tuple(back(momentum, gradient, proj, x, zown))


def solution(mesh):
    return jax.shard_map(
        local,
        mesh=mesh,
        in_specs=(P("fsdp", "tp"), P("fsdp", "tp"), P("fsdp", "tp")),
        out_specs=(P("fsdp", "tp"), P("fsdp", "tp"), P("fsdp", "tp")),
        check_vma=False,
    )
```

time: 587 us -> 186 us (0.32)
  waiting for transfers between devices: 474 us -> 0 us
  Pallas kernels: 0 us -> 117 us
  blocking collectives: 16.4 us -> 0 us
  between operations: 15.2 us -> 1.33 us
  matrix products: 11.7 us -> 1.31 us
    psum x3 -> x0, waiting for transfers between devices: 386 us -> none  [the longest x1 165 us: local(): back_factor = lax.psum(partial_back, 'fsdp')]
    pallas_call x0 -> x3, Pallas kernels: none -> 117 us  [the longest x1 81.3 us: project(): pl.pallas_call(project_kernel, out_shape=[jax.ShapeDtypeStruct((ROWS, RAN...]
    all_gather x1 -> x0, waiting for transfers between devices: 87.7 us -> none  [local(): lax.all_gather(basis_rows, 'fsdp', axis=0, tiled=True)]
    psum x1 -> x0, blocking collectives: 16.4 us -> none  [local(): column_squares = lax.psum(jnp.sum(back_factor * back_factor, axis=1), 'tp')]
    dot_general x5 -> x0, matrix products: 10.4 us -> none  [the longest x1 2.89 us: local(): lax.dot_general(buffer, lax.all_gather(basis_rows, 'fsdp', axis=0, tiled=...]
    another operation x9 -> x10, other arithmetic: 53.7 us -> 53.7 us  [the longest x6 34 us: direct(): lower_factor = jnp.linalg.cholesky(gram)]
  transfers between devices with their start and end apart: 4 -> 0, of which waited for: 4 -> 0; matrix products, arithmetic and copies ran while one was open for 0% -> 0% of each run, Pallas kernels for 0% -> 0%
where the time goes in v2:
time: 186 us; the launch traced here: 183 us
  Pallas kernels  117 us (63%)
  other arithmetic  53.8 us (29%)
  local copies, waits for them, and re-layouts  7.93 us (4%)
  loops' own time  2.14 us (1%)
    pallas_call x1, Pallas kernels, project(): pl.pallas_call(project_kernel, out_shape=[jax.ShapeDtypeStruct((ROWS, RAN...  81.3 us
    another operation x6, other arithmetic, direct(): lower_factor = jnp.linalg.cholesky(gram)  34 us
    pallas_call x1, Pallas kernels, back(): pl.pallas_call(back_kernel, out_shape=[jax.ShapeDtypeStruct((ROWS, COLS),...  30.7 us
    another operation x4, other arithmetic, direct(): lax.linalg.triangular_solve(lower_factor, jnp.eye(RANK, dtype=F32), left_...  19.7 us
    pallas_call x1, Pallas kernels, invert(): pl.pallas_call(invert_kernel, out_shape=[jax.ShapeDtypeStruct((RANK, RANK...  4.72 us
    another operation x6, local copies, waits for them, and re-layouts  3.93 us
    unnamed x7, local copies, waits for them, and re-layouts  3.78 us

profile of v2, /device:TPU:1, one launch (start us, length us, event | category | flops | bytes accessed | tf_op | source)
XLA Modules:
  0.0 183.2 jit_solution(7247492912461370129)
XLA Ops:
  0.6 81.3 %project.1 = (f32[128,256]{1,0:T(8,128)}, f32[256,256]{1,0:T(8,128)S(1)}, f32[56,256]{1,0:T(8,128)}) custom-call(bf16[128,3584]{1,0:T(8,128)(2,1)} %m_ref.3, bf16[128,3584]{1,0:T(8,128)(2,1)} %g_ref.3, bf16[4,3584]{1,0:T(4,128)(2,1)} %basis_ref.1), custom_call_target="tpu_custom_call" | custom-call | tf_op jit(solution)/shard_map/project/pallas_call | solution.py:539
  81.9 4.7 %invert.1 = (f32[256,256]{1,0:T(8,128)S(1)}, f32[1]{0:T(128)}) custom-call(f32[256,256]{1,0:T(8,128)S(1)} %get-tuple-element.14.gram_ref), custom_call_target="tpu_custom_call" | custom-call | tf_op jit(solution)/shard_map/invert/pallas_call | solution.py:573
  87.3 61.4 %conditional.1 = (f32[256,256]{1,0:T(8,128)S(1)}) conditional(s32[]{:T(128)} %bitcast.5, (f32[256,256]{1,0:T(8,128)S(1)}) %tuple.16, f32[256,256]{1,0:T(8,128)S(1)} %get-tuple-element.16), branch_computations={%region_0.5_spmd, %region_5.6_spmd} | conditional | flops 202064128 | bytes 4720855 | solution.py:619
  87.5 0.1 triangular_solve.11
  87.6 0.1 copy.8
  87.8 11.7 %cholesky.5 = f32[128,128]{1,0:T(8,128)S(1)} custom-call(f32[128,128]{1,0:T(8,128)S(1)} %cholesky.46), custom_call_target="Cholesky" | custom-call | tf_op jit(solution)/shard_map/cond/branch_0_fun/jit(cholesky)/cholesky | solution.py:612
  99.5 9.8 %custom-call.12 = f32[1,128,128]{1,2,0:T(8,128)S(1)} custom-call(f32[1,128,128]{2,1,0:T(8,128)S(1)} %get-tuple-element.40), custom_call_target="InvertDiagBlocksLowerTriangular" | custom-call | tf_op jit(solution)/shard_map/cond/branch_0_fun/jit(cholesky)/cholesky | solution.py:612
  109.4 0.2 constant_dynamic-update-slice_fusion.1
  109.6 0.3 convolution_subtract_fusion.1
  109.9 11.7 %cholesky.29 = f32[128,128]{1,0:T(8,128)S(1)} custom-call(f32[128,128]{1,0:T(8,128)S(1)} %convolution_subtract_fusion.1), custom_call_target="Cholesky" | custom-call | tf_op jit(solution)/shard_map/cond/branch_0_fun/jit(cholesky)/cholesky | solution.py:612
  121.6 0.7 compare_reduce_fusion
  123.6 4.2 %while.1 = (s32[]{:T(128)}, f32[256,256]{1,0:T(8,128)S(1)}, s32[2,2]{1,0:T(2,128)S(1)}, f32[2,128,128]{2,1,0:T(8,128)S(1)}, s32[]{:T(128)}) while((s32[]{:T(128)}, f32[256,256]{1,0:T(8,128)S(1)}, s32[2,2]{1,0:T(2,128)S(1)}, f32[2,128,128]{2,1,0:T(8,128)S(1)}, s32[]{:T(128)}) %tuple.32), condition=%wide.while_cond, body=%wide.while_body.sunk | while | flops 2 | bytes 131189 | solution.py:613
  123.9 0.6 fusion.14
  124.5 1.4 bitcast_dynamic-update-slice_fusion.2
  125.9 0.6 fusion.14
  126.4 1.4 bitcast_dynamic-update-slice_fusion.2
  127.8 19.7 %custom-call.13 = f32[2,128,128]{1,2,0:T(8,128)S(1)} custom-call(f32[2,128,128]{2,1,0:T(8,128)S(1)} %get-tuple-element.25), custom_call_target="InvertDiagBlocksLowerTriangular" | custom-call | tf_op jit(solution)/shard_map/cond/branch_0_fun/triangular_solve | solution.py:613
  147.5 0.3 fusion.1
  147.8 0.3 convolution_subtract_fusion
  148.1 0.3 fusion.4
  148.7 30.7 %back.1 = (bf16[128,3584]{1,0:T(8,128)(2,1)}, bf16[4,3584]{1,0:T(4,128)(2,1)}, bf16[128,3584]{1,0:T(8,128)(2,1)}) custom-call(bf16[128,3584]{1,0:T(8,128)(2,1)} %m_ref.3, bf16[128,3584]{1,0:T(8,128)(2,1)} %g_ref.3, f32[128,256]{1,0:T(8,128)} %get-tuple-element.13.proj_ref, f32[256,256]{1,0:T(8,128)S(1)} %get-tuple-element.95.x_ref, ...), custom_call_target="tpu_custom_call" | custom-call | tf_op jit(solution)/shard_map/back/pallas_call | solution.py:585
  179.4 0.0 copy-start.1
  179.4 0.0 copy-start
  179.4 2.2 %copy.26 = bf16[128,3584]{1,0:T(8,128)(2,1)} copy(bf16[128,3584]{1,0:T(8,128)(2,1)} %get-tuple-element.92) | data formatting | bytes 1835008
  181.7 0.0 copy-done.1
  181.7 0.6 copy.27
  182.3 0.0 copy-done
  182.3 0.9 copy.28
  (12 shorter events, 0.2 us)
Async XLA Ops:
  179.4 2.3 %copy-start.1 = (bf16[4,3584]{1,0:T(4,128)(2,1)S(1)}, bf16[4,3584]{1,0:T(4,128)(2,1)}, u32[]{:S(2)}) copy-start(bf16[4,3584]{1,0:T(4,128)(2,1)} %get-tuple-element.93) | copy-start | bytes 86020
  179.4 2.9 %copy-start = (bf16[128,3584]{1,0:T(8,128)(2,1)S(1)}, bf16[128,3584]{1,0:T(8,128)(2,1)}, u32[]{:S(2)}) copy-start(bf16[128,3584]{1,0:T(8,128)(2,1)} %get-tuple-element.94) | copy-start | bytes 2752516

commit v3 on v2

--- a/solution.py
+++ b/solution.py
@@ -63,10 +63,16 @@
         pl.semaphore_signal(barrier, inc=1, device_id=(mod8(y + k) * NZ + z, t), device_id_type=MESH)
         pl.semaphore_signal(barrier, inc=1, device_id=(y * NZ + mod8(z + k), t), device_id_type=MESH)
         pl.semaphore_signal(barrier, inc=1, device_id=(f, mod8(t + k)), device_id_type=MESH)
-    pl.semaphore_wait(barrier, 21)
-
-
-ORDER = (0, 1, 3, 2)
+
+
+def met():
+    pl.semaphore_wait(pltpu.get_barrier_semaphore(), 21)
+
+
+WAVE = (
+    (0, None), (1, None), (3, None), (0, 0), (2, None), (1, 0), (3, 0), (0, 1), (2, 0), (1, 1), (3, 1), (0, 2),
+    (2, 1), (1, 2), (3, 2), (0, 3), (2, 2), (1, 3), (3, 3), (2, 3),
+)
 
 
 def fourth(d, i):
@@ -120,7 +126,7 @@
     for k in (1, 7, 2, 6, 3, 5, 4):
         straight(k, (line(even, y, z, k), t)).start()
     between[0]()
-    for r in ORDER:
+    for r, h in WAVE:
         for ax in range(2):
             i = lax.rem(half[ax] + r, 4)
 
@@ -133,31 +139,29 @@
                 for d in range(2):
                     send(ax, d, i, 0)
 
-            if r == 0:
-                pl.when(jnp.logical_not(home[ax]))(first)
-            else:
-                first()
-    between[1]()
-    for h in range(4):
-        for r in ORDER:
-            for ax in range(2):
-                i = lax.rem(half[ax] + r, 4)
-                for d in range(2):
-                    if h < 2:
-                        landed(ax, d, i, h)
-                        send(ax, d, i, h + 1)
-                    elif h == 2:
-                        landed(ax, d, i, h)
-
-                        @pl.when(fourth(d, i))
-                        def _():
-                            send(ax, d, i, 3)
-                    else:
-
-                        @pl.when(fourth(d, i))
-                        def _():
-                            landed(ax, d, i, 3)
-        between[h + 2]()
+            if h is None:
+                if r == 0:
+                    pl.when(jnp.logical_not(home[ax]))(first)
+                else:
+                    first()
+                continue
+            for d in range(2):
+                if h < 2:
+                    landed(ax, d, i, h)
+                    send(ax, d, i, h + 1)
+                elif h == 2:
+                    landed(ax, d, i, h)
+
+                    @pl.when(fourth(d, i))
+                    def _():
+                        send(ax, d, i, 3)
+                else:
+
+                    @pl.when(fourth(d, i))
+                    def _():
+                        landed(ax, d, i, 3)
+        if r == 2:
+            between[1 if h is None else h + 2]()
 
     def finish():
         for k in range(1, 8):
@@ -201,6 +205,85 @@
         ).wait_recv()
 
 
+def start_inverse(gram, sx):
+    i = lax.broadcasted_iota(jnp.int32, (RANK, RANK), 0)
+    j = lax.broadcasted_iota(jnp.int32, (RANK, RANK), 1)
+    on = jnp.where(i == j, gram, 0.0)
+    down = lax.rsqrt(jnp.sum(on, axis=1, keepdims=True))
+    across = lax.rsqrt(jnp.sum(on, axis=0, keepdims=True))
+    sx[:, :RANK] = gram * down * across
+    sx[:, RANK:] = jnp.where(i == j, down, 0.0)
+
+
+def step_inverse(sx):
+    i = lax.broadcasted_iota(jnp.int32, (RANK, RANK), 0)
+    j = lax.broadcasted_iota(jnp.int32, (RANK, RANK), 1)
+    e = sx[:, :RANK] - jnp.where(i == j, 1.0, 0.0)
+    w = jnp.where(i > j, -e, jnp.where(i == j, 1.0 - 0.5 * e, 0.0))
+    out = jnp.dot(w, sx[...], precision=HIGHEST, preferred_element_type=F32)
+    sx[:, RANK:] = out[:, RANK:]
+    sx[:, :RANK] = lax.dot_general(
+        out[:, :RANK], w, (((1,), (1,)), ((), ())), precision=HIGHEST, preferred_element_type=F32
+    )
+
+
+def missed(sx):
+    i = lax.broadcasted_iota(jnp.int32, (RANK, RANK), 0)
+    j = lax.broadcasted_iota(jnp.int32, (RANK, RANK), 1)
+    e = sx[:, :RANK] - jnp.where(i == j, 1.0, 0.0)
+    return jnp.sum(e * e, axis=0, keepdims=True)
+
+
+def spread(zown, x, proj, low_ref, back_ref, sq_ref, place_, q1, q2, q3, sems, ready):
+    f, t, y, z, even = place_
+    s1, r1, s2, r2, e1, f1, e2, f2, e3, f3 = sems
+    me = own_slot(even, y, z)
+    tp_id = lambda p: (f, p)
+    y_id = lambda p: (p * NZ + z, t)
+    z_id = lambda p: (y * NZ + p, t)
+    turn = (((1,), (1,)), ((), ()))
+    mine = lax.dot_general(zown, x(), turn, precision=HIGHEST, preferred_element_type=F32)
+    back_ref[pl.ds(pl.multiple_of(me * PAD, PAD), PAD), :] = jnp.concatenate(
+        [mine, jnp.zeros((PAD - CUT, RANK), F32)], axis=0
+    ).astype(BF16)
+    q1[t] = jnp.broadcast_to(jnp.sum(mine * mine, axis=0, keepdims=True), (8, RANK))
+    ready()
+    waits = []
+
+    def open_squares():
+        waits.extend(exchange(lambda p: q1.at[t], lambda p: q1.at[p], tp_id, t, e1, f1))
+        low_ref[...] = lax.dot_general(
+            proj(), x(), turn, precision=HIGHEST, preferred_element_type=F32
+        ).astype(BF16)
+
+    def fold(buf):
+        sums = buf[0]
+        for p in range(1, 8):
+            sums = sums + buf[p]
+        return sums
+
+    def over_y():
+        arrived(lambda p: q1.at[p], tp_id, t, e1, f1)
+        q2[y] = fold(q1)
+        waits.extend(exchange(lambda p: q2.at[y], lambda p: q2.at[p], y_id, y, e2, f2))
+
+    def over_z():
+        arrived(lambda p: q2.at[p], y_id, y, e2, f2)
+        q3[z] = fold(q2)
+        waits.extend(exchange(lambda p: q3.at[z], lambda p: q3.at[p], z_id, z, e3, f3))
+
+    nothing = lambda: None
+    finish = gather(
+        back_ref, PAD, f, t, y, z, even, s1, r1, s2, r2,
+        [open_squares, over_y, over_z, nothing, nothing, nothing],
+    )
+    arrived(lambda p: q3.at[p], z_id, z, e3, f3)
+    sq_ref[...] = fold(q3)
+    finish()
+    for copy in waits:
+        copy.wait_send()
+
+
 def thirds(v):
     a1 = v.astype(BF16)
     rest = v - a1.astype(F32)
@@ -209,9 +292,10 @@
 
 
 def project_kernel(
-    m_ref, g_ref, basis_ref, proj_ref, gram_ref, z_ref,
-    vbuf, bbuf, mbuf, gbuf, stage, sel, part, tbuf, gpart, ybuf, zbuf, work, land, near, far,
-    local_sem, s1, r1, s2, r2, s3, r3, s4, r4, ps, pr, as_, ar, ys, yr, zs, zr, bs, br, ts, tr,
+    m_ref, g_ref, basis_ref, proj_ref, gram_ref, z_ref, err_ref, low_ref, back_ref, sq_ref,
+    vbuf, bbuf, mbuf, gbuf, stage, sel, part, tbuf, gpart, ybuf, zbuf, work, land, near, far, sx, q1, q2, q3,
+    local_sem, s1, r1, s2, r2, s3, r3, s4, r4, s5, r5, s6, r6, ps, pr, as_, ar, ys, yr, zs, zr, bs, br, ts, tr,
+    e1, f1, e2, f2, e3, f3,
 ):
     f, t, y, z, even = place()
     me = own_slot(even, y, z)
@@ -223,11 +307,12 @@
     cb.start()
     cm.start()
     cg.start()
+    greet(f, t, y, z)
     cb.wait()
     own = stage[...].astype(F32)
     pieces = [own[:, j * PC:(j + 1) * PC] for j in range(PARTS)]
     vbuf[pl.ds(pl.multiple_of(me * SLOT, SLOT), SLOT), :] = jnp.concatenate(pieces, axis=0).astype(BF16)
-    greet(f, t, y, z)
+    met()
 
     def prepare():
         cm.wait()
@@ -392,6 +477,14 @@
                 far[at[1 - ax]] = both
 
     arrived(lambda p: gram_ref.at[block(p)], tp_id, t, ts, tr)
+    start_inverse(gram_ref[...], sx)
+
+    def advance(i, carry):
+        step_inverse(sx)
+        return carry
+
+    lax.fori_loop(0, 6, advance, 0)
+    err_ref[...] = missed(sx)
     for k in range(1, 8):
         p = mod8(spot + k)
         pltpu.make_async_remote_copy(
@@ -402,6 +495,11 @@
     for p in range(1, 8):
         sums = sums + far[p]
     z_ref[...] = sums
+    sems = (s5, r5, s6, r6, e1, f1, e2, f2, e3, f3)
+    spread(
+        sums, lambda: sx[:, RANK:], lambda: proj_ref[...], low_ref, back_ref, sq_ref, (f, t, y, z, even), q1, q2, q3, sems,
+        lambda: None,
+    )
     finish()
     for copies in (c1, c2, c3, c4, c5, c6, sent):
         for copy in copies:
@@ -413,119 +511,35 @@
                 cross(ax, i, aside).wait_send()
 
 
-def invert_kernel(gram_ref, x_ref, err_ref, sx):
-    i = lax.broadcasted_iota(jnp.int32, (RANK, RANK), 0)
-    j = lax.broadcasted_iota(jnp.int32, (RANK, RANK), 1)
-    diagonal = i == j
-    gram = gram_ref[...]
-    on = jnp.where(diagonal, gram, 0.0)
-    down = lax.rsqrt(jnp.sum(on, axis=1, keepdims=True))
-    across = lax.rsqrt(jnp.sum(on, axis=0, keepdims=True))
-    sx[:, :RANK] = gram * down * across
-    sx[:, RANK:] = jnp.where(diagonal, down, 0.0)
-
-    def miss():
-        return jnp.max(jnp.abs(sx[:, :RANK] - jnp.where(diagonal, 1.0, 0.0)))
-
-    def more(state):
-        count, err = state
-        return jnp.logical_and(count < 16, err > 1e-5)
-
-    def step(state):
-        count, _ = state
-        e = sx[:, :RANK] - jnp.where(diagonal, 1.0, 0.0)
-        w = jnp.where(i > j, -e, jnp.where(diagonal, 1.0 - 0.5 * e, 0.0))
-        out = jnp.dot(w, sx[...], precision=HIGHEST, preferred_element_type=F32)
-        sx[:, RANK:] = out[:, RANK:]
-        sx[:, :RANK] = lax.dot_general(
-            out[:, :RANK], w, (((1,), (1,)), ((), ())), precision=HIGHEST, preferred_element_type=F32
-        )
-        return count + 1, miss()
-
-    _, err = lax.while_loop(more, step, (jnp.int32(0), miss()))
-    x_ref[...] = sx[:, RANK:]
-    err_ref[0] = err
-
-
-def back_kernel(
-    m_ref, g_ref, proj_ref, x_ref, z_ref, mom_ref, own_ref, upd_ref,
-    mbuf, gbuf, bbuf, obuf, qbuf, tbuf, ybuf, zbuf,
-    local_sem, s1, r1, s2, r2, ts, tr, ys, yr, zs, zr,
+def again_kernel(
+    proj_ref, x_ref, z_ref, low_ref, back_ref, sq_ref, q1, q2, q3, s1, r1, s2, r2, e1, f1, e2, f2, e3, f3
 ):
-    f, t, y, z, even = place()
-    me = own_slot(even, y, z)
-    cm = pltpu.make_async_copy(m_ref, mbuf, local_sem.at[0])
-    cg = pltpu.make_async_copy(g_ref, gbuf, local_sem.at[1])
-    cm.start()
-    cg.start()
-    tp_id = lambda p: (f, p)
-    y_id = lambda p: (p * NZ + z, t)
-    z_id = lambda p: (y * NZ + p, t)
-    mine = lax.dot_general(
-        z_ref[...], x_ref[...], (((1,), (1,)), ((), ())), precision=HIGHEST, preferred_element_type=F32
-    )
-    obuf[pl.ds(pl.multiple_of(me * PAD, PAD), PAD), :] = jnp.concatenate(
-        [mine, jnp.zeros((PAD - CUT, RANK), F32)], axis=0
-    ).astype(BF16)
-    tbuf[t] = jnp.broadcast_to(jnp.sum(mine * mine, axis=0, keepdims=True), (8, RANK))
-    greet(f, t, y, z)
-    waits = []
-
-    def open_squares():
-        waits.extend(exchange(lambda p: tbuf.at[t], lambda p: tbuf.at[p], tp_id, t, ts, tr))
-        cm.wait()
-        cg.wait()
-        for j in range(PARTS):
-            cols = slice(j * PC, (j + 1) * PC)
-            bbuf[:, cols] = (mbuf[:, cols].astype(F32) + gbuf[:, cols].astype(F32)).astype(BF16)
-        qbuf[...] = lax.dot_general(
-            proj_ref[...], x_ref[...], (((1,), (1,)), ((), ())), precision=HIGHEST, preferred_element_type=F32
-        ).astype(BF16)
-
-    def fold(buf):
-        sums = buf[0]
-        for p in range(1, 8):
-            sums = sums + buf[p]
-        return sums
-
-    def over_y():
-        arrived(lambda p: tbuf.at[p], tp_id, t, ts, tr)
-        ybuf[y] = fold(tbuf)
-        waits.extend(exchange(lambda p: ybuf.at[y], lambda p: ybuf.at[p], y_id, y, ys, yr))
-
-    def over_z():
-        arrived(lambda p: ybuf.at[p], y_id, y, ys, yr)
-        zbuf[z] = fold(ybuf)
-        waits.extend(exchange(lambda p: zbuf.at[z], lambda p: zbuf.at[p], z_id, z, zs, zr))
-
-    nothing = lambda: None
-    finish = gather(
-        obuf, PAD, f, t, y, z, even, s1, r1, s2, r2,
-        [open_squares, over_y, over_z, nothing, nothing, nothing],
-    )
-    arrived(lambda p: zbuf.at[p], z_id, z, zs, zr)
-    squares = fold(zbuf)[0:1, :] + epsilon
-    inverse = lax.rsqrt(squares)
-    low = qbuf[...]
+    where = place()
+    greet(*where[:4])
+    sems = (s1, r1, s2, r2, e1, f1, e2, f2, e3, f3)
+    spread(
+        z_ref[...], lambda: x_ref[...], lambda: proj_ref[...], low_ref, back_ref, sq_ref, where, q1, q2, q3, sems, met
+    )
+
+
+def output_kernel(m_ref, g_ref, low_ref, back_ref, sq_ref, mom_ref, own_ref, upd_ref):
+    f = lax.axis_index("fsdp")
+    squares = sq_ref[0:1, :] + epsilon
+    low = low_ref[...]
     scaled = (low.astype(F32) * jnp.sqrt(squares).astype(BF16).astype(F32)).astype(BF16)
     pick = jnp.where(
         lax.broadcasted_iota(jnp.int32, (8, RANK), 0) + f * OWN == lax.broadcasted_iota(jnp.int32, (8, RANK), 1),
         1.0, 0.0,
     ).astype(BF16)
     turn = (((1,), (1,)), ((), ()))
-    for j in range(PARTS):
-        cols = slice(j * PC, (j + 1) * PC)
-        pieces = [obuf[s * PAD:s * PAD + CUT, :].astype(F32) for s in range(j * 16, (j + 1) * 16)]
-        nb = (jnp.concatenate(pieces, axis=0) * inverse).astype(BF16)
-        own_ref[:, cols] = lax.dot_general(pick, nb, turn, preferred_element_type=F32)[0:OWN].astype(BF16)
-        upd_ref[:, cols] = (UNIT * lax.dot_general(low, nb, turn, preferred_element_type=F32)).astype(BF16)
-        mom_ref[:, cols] = (
-            bbuf[:, cols].astype(F32)
-            - (1.0 - momentum_decay) * lax.dot_general(scaled, nb, turn, preferred_element_type=F32)
-        ).astype(BF16)
-    finish()
-    for copy in waits:
-        copy.wait_send()
+    pieces = [back_ref[s * PAD:s * PAD + CUT, :].astype(F32) for s in range(16)]
+    nb = (jnp.concatenate(pieces, axis=0) * lax.rsqrt(squares)).astype(BF16)
+    buffer = (m_ref[...].astype(F32) + g_ref[...].astype(F32)).astype(BF16).astype(F32)
+    own_ref[...] = lax.dot_general(pick, nb, turn, preferred_element_type=F32)[0:OWN].astype(BF16)
+    upd_ref[...] = (UNIT * lax.dot_general(low, nb, turn, preferred_element_type=F32)).astype(BF16)
+    mom_ref[...] = (
+        buffer - (1.0 - momentum_decay) * lax.dot_general(scaled, nb, turn, preferred_element_type=F32)
+    ).astype(BF16)
 
 
 VMEM = pl.BlockSpec(memory_space=pltpu.VMEM)
@@ -533,6 +547,11 @@
 DMA = pltpu.SemaphoreType.DMA
 LIMIT = 56 * 2**20
 WIDE = (2, 2, 4, 4)
+SPREAD = [
+    jax.ShapeDtypeStruct((ROWS, RANK), BF16),
+    jax.ShapeDtypeStruct((NF * PAD, RANK), BF16),
+    jax.ShapeDtypeStruct((8, RANK), F32),
+]
 
 
 def project(momentum, gradient, basis_rows):
@@ -542,9 +561,10 @@
             jax.ShapeDtypeStruct((ROWS, RANK), F32),
             jax.ShapeDtypeStruct((RANK, RANK), F32),
             jax.ShapeDtypeStruct((CUT, RANK), F32),
-        ],
+            jax.ShapeDtypeStruct((1, RANK), F32),
+        ] + SPREAD,
         in_specs=[HBM, HBM, HBM],
-        out_specs=[VMEM, VMEM, VMEM],
+        out_specs=[VMEM] * 7,
         scratch_shapes=[
             pltpu.VMEM((NF * SLOT, PC), BF16),
             pltpu.VMEM((ROWS, COLS), BF16),
@@ -561,51 +581,54 @@
             pltpu.VMEM(WIDE + (CUT, RANK), F32),
             pltpu.VMEM((2, 4, CUT, RANK), F32),
             pltpu.VMEM((8, CUT, RANK), F32),
+            pltpu.VMEM((RANK, 2 * RANK), F32),
+            pltpu.VMEM((8, 8, RANK), F32),
+            pltpu.VMEM((8, 8, RANK), F32),
+            pltpu.VMEM((8, 8, RANK), F32),
             DMA((3,)),
             DMA((8,)), DMA((8,)), DMA(WIDE), DMA(WIDE), DMA(WIDE), DMA(WIDE), DMA((2, 4)), DMA((8,)),
-        ] + [DMA((8,))] * 12,
+            DMA((8,)), DMA((8,)), DMA(WIDE), DMA(WIDE),
+        ] + [DMA((8,))] * 18,
         compiler_params=pltpu.CompilerParams(collective_id=0, has_side_effects=True, vmem_limit_bytes=LIMIT),
         name="project",
     )(momentum, gradient, basis_rows)
 
 
-def invert(gram):
+def again(proj, x, zown):
     return pl.pallas_call(
-        invert_kernel,
-        out_shape=[jax.ShapeDtypeStruct((RANK, RANK), F32), jax.ShapeDtypeStruct((1,), F32)],
-        in_specs=[VMEM],
-        out_specs=[VMEM, pl.BlockSpec(memory_space=pltpu.SMEM)],
-        scratch_shapes=[pltpu.VMEM((RANK, 2 * RANK), F32)],
-        compiler_params=pltpu.CompilerParams(vmem_limit_bytes=LIMIT),
-        name="invert",
-    )(gram)
-
-
-def back(momentum, gradient, proj, x, zown):
+        again_kernel,
+        out_shape=SPREAD,
+        in_specs=[VMEM] * 3,
+        out_specs=[VMEM] * 3,
+        scratch_shapes=[pltpu.VMEM((8, 8, RANK), F32)] * 3
+        + [DMA((8,)), DMA((8,)), DMA(WIDE), DMA(WIDE)]
+        + [DMA((8,))] * 6,
+        compiler_params=pltpu.CompilerParams(collective_id=1, has_side_effects=True, vmem_limit_bytes=LIMIT),
+        name="again",
+    )(proj, x, zown)
+
+
+def outputs(momentum, gradient, low, back, squares):
+    tall = pl.BlockSpec((ROWS, PC), lambda j: (0, j))
     return pl.pallas_call(
-        back_kernel,
+        output_kernel,
         out_shape=[
             jax.ShapeDtypeStruct((ROWS, COLS), BF16),
             jax.ShapeDtypeStruct((OWN, COLS), BF16),
             jax.ShapeDtypeStruct((ROWS, COLS), BF16),
         ],
-        in_specs=[HBM, HBM, VMEM, VMEM, VMEM],
-        out_specs=[VMEM, VMEM, VMEM],
-        scratch_shapes=[
-            pltpu.VMEM((ROWS, COLS), BF16),
-            pltpu.VMEM((ROWS, COLS), BF16),
-            pltpu.VMEM((ROWS, COLS), BF16),
-            pltpu.VMEM((NF * PAD, RANK), BF16),
-            pltpu.VMEM((ROWS, RANK), BF16),
-            pltpu.VMEM((8, 8, RANK), F32),
-            pltpu.VMEM((8, 8, RANK), F32),
-            pltpu.VMEM((8, 8, RANK), F32),
-            DMA((2,)),
-            DMA((8,)), DMA((8,)), DMA(WIDE), DMA(WIDE),
-        ] + [DMA((8,))] * 6,
-        compiler_params=pltpu.CompilerParams(collective_id=1, has_side_effects=True, vmem_limit_bytes=LIMIT),
-        name="back",
-    )(momentum, gradient, proj, x, zown)
+        grid=(PARTS,),
+        in_specs=[
+            tall,
+            tall,
+            pl.BlockSpec((ROWS, RANK), lambda j: (0, 0)),
+            pl.BlockSpec((16 * PAD, RANK), lambda j: (j, 0)),
+            pl.BlockSpec((8, RANK), lambda j: (0, 0)),
+        ],
+        out_specs=[tall, pl.BlockSpec((OWN, PC), lambda j: (0, j)), tall],
+        compiler_params=pltpu.CompilerParams(vmem_limit_bytes=LIMIT),
+        name="outputs",
+    )(momentum, gradient, low, back, squares)
 
 
 def direct(gram):
@@ -614,10 +637,14 @@
 
 
 def local(momentum, gradient, basis_rows):
-    proj, gram, zown = project(momentum, gradient, basis_rows)
-    x, err = invert(gram)
-    x = lax.cond(err[0] < 1e-5, lambda g, v: v, lambda g, v: direct(g), gram, x)
-    return tuple(back(momentum, gradient, proj, x, zown))
+    proj, gram, zown, err, low, back, squares = project(momentum, gradient, basis_rows)
+    low, back, squares = lax.cond(
+        jnp.sum(err) < 1e-8,
+        lambda proj, gram, zown, *now: now,
+        lambda proj, gram, zown, *now: tuple(again(proj, direct(gram), zown)),
+        proj, gram, zown, low, back, squares,
+    )
+    return tuple(outputs(momentum, gradient, low, back, squares))
 
 
 def solution(mesh):

time: 186 us -> 207 us (1.11)
  Pallas kernels: 117 us -> 138 us
  local copies, waits for them, and re-layouts: 7.93 us -> 4.28 us
    pallas_call x1, Pallas kernels: 81.3 us -> 104 us  [project(): pl.pallas_call(project_kernel, out_shape=[jax.ShapeDtypeStruct((ROWS, RAN...]
    unnamed x7 -> x0, local copies, waits for them, and re-layouts: 3.78 us -> none
    another operation x6 -> x7, local copies, waits for them, and re-layouts: 3.93 us -> 4.19 us
where the time goes in v3:
time: 207 us; the launch traced here: 203 us
  Pallas kernels  138 us (67%)
  other arithmetic  55.8 us (27%)
  local copies, waits for them, and re-layouts  4.28 us (2%)
  loops' own time  2.19 us (1%)
    pallas_call x1, Pallas kernels, project(): pl.pallas_call(project_kernel, out_shape=[jax.ShapeDtypeStruct((ROWS, RAN...  104 us
    another operation x6, other arithmetic, direct(): lower_factor = jnp.linalg.cholesky(gram)  34 us
    pallas_call x1, Pallas kernels, again(): pl.pallas_call(again_kernel, out_shape=SPREAD, in_specs=[VMEM] * 3, out_s...  29.5 us
    another operation x4, other arithmetic, direct(): lax.linalg.triangular_solve(lower_factor, jnp.eye(RANK, dtype=F32), left_...  20.4 us
    pallas_call x1, Pallas kernels, outputs(): pl.pallas_call(output_kernel, out_shape=[jax.ShapeDtypeStruct((ROWS, COLS...  4.66 us
    another operation x7, local copies, waits for them, and re-layouts  4.19 us

profile of v3, /device:TPU:1, one launch (start us, length us, event | category | flops | bytes accessed | tf_op | source)
XLA Modules:
  0.0 203.0 jit_solution(10683192084241434963)
XLA Ops:
  0.6 104.0 %project.1 = (f32[128,256]{1,0:T(8,128)S(1)}, f32[256,256]{1,0:T(8,128)S(1)}, f32[56,256]{1,0:T(8,128)S(1)}, f32[1,256]{1,0:T(1,128)}, bf16[128,256]{1,0:T(8,128...) custom-call(bf16[128,3584]{1,0:T(8,128)(2,1)} %m_ref.3, bf16[128,3584]{1,0:T(8,128)(2,1)} %g_ref.3, ...), custom_call_target="tpu_custom_call" | custom-call | tf_op jit(solution)/shard_map/project/pallas_call | solution.py:558
  104.6 1.3 reduce_sum.9
  106.6 91.8 %conditional.1 = ((bf16[128,256]{1,0:T(8,128)(2,1)S(1)}, bf16[4096,256]{1,0:T(8,128)(2,1)S(1)}, f32[8,256]{1,0:T(8,128)S(1)})) conditional(s32[]{:T(128)} %convert_element_type.4, (f32[256,256]{1,0:T(8,128)S(1)}, f32[128,256]{1,0:T(8,128)S(1)}, f32[56,256]{1,0:T(8,128)S(1)}) %tuple.13, (bf16[128,256]{1,0:T(8,128)(2,1)S(1)}, ...), branch_computations={%region_1.6_spmd, %region_6.7_spmd} | conditional | flops 202064128 | bytes 4720855 | solution.py:641
  106.8 0.1 triangular_solve.11
  106.9 0.1 copy.7
  107.1 11.7 %cholesky.5 = f32[128,128]{1,0:T(8,128)S(1)} custom-call(f32[128,128]{1,0:T(8,128)S(1)} %cholesky.46), custom_call_target="Cholesky" | custom-call | tf_op jit(solution)/shard_map/cond/branch_0_fun/jit(cholesky)/cholesky | solution.py:635
  118.8 9.8 %custom-call.12 = f32[1,128,128]{1,2,0:T(8,128)S(1)} custom-call(f32[1,128,128]{2,1,0:T(8,128)S(1)} %get-tuple-element.62), custom_call_target="InvertDiagBlocksLowerTriangular" | custom-call | tf_op jit(solution)/shard_map/cond/branch_0_fun/jit(cholesky)/cholesky | solution.py:635
  128.7 0.2 constant_dynamic-update-slice_fusion.1
  128.9 0.3 convolution_subtract_fusion.1
  129.2 11.7 %cholesky.29 = f32[128,128]{1,0:T(8,128)S(1)} custom-call(f32[128,128]{1,0:T(8,128)S(1)} %convolution_subtract_fusion.1), custom_call_target="Cholesky" | custom-call | tf_op jit(solution)/shard_map/cond/branch_0_fun/jit(cholesky)/cholesky | solution.py:635
  140.9 0.7 compare_reduce_fusion
  143.0 4.3 %while.1 = (s32[]{:T(128)}, f32[256,256]{1,0:T(8,128)S(1)}, s32[2,2]{1,0:T(2,128)S(1)}, f32[2,128,128]{2,1,0:T(8,128)S(1)}, s32[]{:T(128)}) while((s32[]{:T(128)}, f32[256,256]{1,0:T(8,128)S(1)}, s32[2,2]{1,0:T(2,128)S(1)}, f32[2,128,128]{2,1,0:T(8,128)S(1)}, s32[]{:T(128)}) %tuple.34), condition=%wide.while_cond, body=%wide.while_body.sunk | while | flops 2 | bytes 131189 | solution.py:636
  143.3 0.6 fusion.14
  143.9 1.4 bitcast_dynamic-update-slice_fusion.2
  145.3 0.6 fusion.14
  145.9 1.4 bitcast_dynamic-update-slice_fusion.2
  147.4 19.7 %custom-call.13 = f32[2,128,128]{1,2,0:T(8,128)S(1)} custom-call(f32[2,128,128]{2,1,0:T(8,128)S(1)} %get-tuple-element.45), custom_call_target="InvertDiagBlocksLowerTriangular" | custom-call | tf_op jit(solution)/shard_map/cond/branch_0_fun/triangular_solve | solution.py:636
  167.0 0.3 fusion.1
  167.3 0.3 convolution_subtract_fusion
  167.6 0.3 fusion.4
  167.9 0.7 pad_maximum_fusion.x_ref
  168.6 29.5 %again.1 = (bf16[128,256]{1,0:T(8,128)(2,1)S(1)}, bf16[4096,256]{1,0:T(8,128)(2,1)S(1)}, f32[8,256]{1,0:T(8,128)S(1)}) custom-call(f32[128,256]{1,0:T(8,128)S(1)} %get-tuple-element.12.proj_ref, f32[256,256]{1,0:T(8,128)} %pad_maximum_fusion.x_ref, f32[56,256]{1,0:T(8,128)S(1)} %get-tuple-element.14.z_ref), custom_call_target="tpu_custom_call" | custom-call | tf_op jit(solution)/shard_map/cond/branch_0_fun/again/pallas_call | solution.py:598
  198.4 4.7 %outputs.1 = (bf16[128,3584]{1,0:T(8,128)(2,1)}, bf16[4,3584]{1,0:T(4,128)(2,1)}, bf16[128,3584]{1,0:T(8,128)(2,1)}) custom-call(bf16[128,3584]{1,0:T(8,128)(2,1)} %m_ref.3, bf16[128,3584]{1,0:T(8,128)(2,1)} %g_ref.3, bf16[128,256]{1,0:T(8,128)(2,1)S(1)} %get-tuple-element.35.low_ref, bf16[4096,256]{1,0:T(8,128)(2,1)S(1)} %get-tuple-element.36.back_ref, ...), custom_call_target="tpu_custom_call" | custom-call | tf_op jit(solution)/shard_map/outputs/pallas_call | solution.py:613
  (11 shorter events, 0.2 us)

commit v4 on v3

--- a/solution.py
+++ b/solution.py
@@ -22,7 +22,8 @@
 PC = COLS // PARTS
 SLOT = 16
 CUT = COLS // NF
-PAD = 64
+PACK = 2 * CUT
+HALF = RANK // 2
 
 epsilon = 1e-06
 momentum_decay = 0.95
@@ -231,29 +232,33 @@
     i = lax.broadcasted_iota(jnp.int32, (RANK, RANK), 0)
     j = lax.broadcasted_iota(jnp.int32, (RANK, RANK), 1)
     e = sx[:, :RANK] - jnp.where(i == j, 1.0, 0.0)
-    return jnp.sum(e * e, axis=0, keepdims=True)
-
-
-def spread(zown, x, proj, low_ref, back_ref, sq_ref, place_, q1, q2, q3, sems, ready):
-    f, t, y, z, even = place_
+    return jnp.sum(e * e)
+
+
+def pack(columns):
+    return jnp.concatenate([columns[:, :HALF], columns[:, HALF:]], axis=0).astype(BF16)
+
+
+def spread(zown, sx, proj_ref, check_ref, low_ref, back_ref, sq_ref, where, q1, q2, q3, sems):
+    f, t, y, z, even = where
     s1, r1, s2, r2, e1, f1, e2, f2, e3, f3 = sems
     me = own_slot(even, y, z)
     tp_id = lambda p: (f, p)
     y_id = lambda p: (p * NZ + z, t)
     z_id = lambda p: (y * NZ + p, t)
     turn = (((1,), (1,)), ((), ()))
-    mine = lax.dot_general(zown, x(), turn, precision=HIGHEST, preferred_element_type=F32)
-    back_ref[pl.ds(pl.multiple_of(me * PAD, PAD), PAD), :] = jnp.concatenate(
-        [mine, jnp.zeros((PAD - CUT, RANK), F32)], axis=0
-    ).astype(BF16)
-    q1[t] = jnp.broadcast_to(jnp.sum(mine * mine, axis=0, keepdims=True), (8, RANK))
-    ready()
+    mine = lax.dot_general(zown, sx[:, RANK:], turn, precision=HIGHEST, preferred_element_type=F32)
+    back_ref[pl.ds(pl.multiple_of(me * PACK, 16), PACK), :] = pack(mine)
+    first = lax.broadcasted_iota(jnp.int32, (8, RANK), 0) == 0
+    q1[t] = jnp.where(
+        first, jnp.sum(mine * mine, axis=0, keepdims=True), jnp.sum(zown * zown, axis=0, keepdims=True)
+    )
     waits = []
 
     def open_squares():
         waits.extend(exchange(lambda p: q1.at[t], lambda p: q1.at[p], tp_id, t, e1, f1))
         low_ref[...] = lax.dot_general(
-            proj(), x(), turn, precision=HIGHEST, preferred_element_type=F32
+            proj_ref[...], sx[:, RANK:], turn, precision=HIGHEST, preferred_element_type=F32
         ).astype(BF16)
 
     def fold(buf):
@@ -274,11 +279,15 @@
 
     nothing = lambda: None
     finish = gather(
-        back_ref, PAD, f, t, y, z, even, s1, r1, s2, r2,
+        back_ref, PACK, f, t, y, z, even, s1, r1, s2, r2,
         [open_squares, over_y, over_z, nothing, nothing, nothing],
     )
     arrived(lambda p: q3.at[p], z_id, z, e3, f3)
-    sq_ref[...] = fold(q3)
+    squares = fold(q3)
+    sq_ref[...] = squares
+    x = sx[:, RANK:]
+    grown = lax.dot_general(squares, x * x, turn, precision=HIGHEST, preferred_element_type=F32)[1:2, :]
+    check_ref[1] = jnp.sum(grown / squares[0:1, :]) * (1.0 / RANK)
     finish()
     for copy in waits:
         copy.wait_send()
@@ -292,8 +301,8 @@
 
 
 def project_kernel(
-    m_ref, g_ref, basis_ref, proj_ref, gram_ref, z_ref, err_ref, low_ref, back_ref, sq_ref,
-    vbuf, bbuf, mbuf, gbuf, stage, sel, part, tbuf, gpart, ybuf, zbuf, work, land, near, far, sx, q1, q2, q3,
+    m_ref, g_ref, basis_ref, proj_ref, gram_ref, check_ref, b_ref, low_ref, back_ref, sq_ref,
+    vbuf, mbuf, gbuf, stage, sel, part, tbuf, gpart, ybuf, zbuf, work, land, near, far, sx, q1, q2, q3,
     local_sem, s1, r1, s2, r2, s3, r3, s4, r4, s5, r5, s6, r6, ps, pr, as_, ar, ys, yr, zs, zr, bs, br, ts, tr,
     e1, f1, e2, f2, e3, f3,
 ):
@@ -319,7 +328,7 @@
         cg.wait()
         for j in range(PARTS):
             cols = slice(j * PC, (j + 1) * PC)
-            bbuf[:, cols] = (mbuf[:, cols].astype(F32) + gbuf[:, cols].astype(F32)).astype(BF16)
+            b_ref[:, cols] = (mbuf[:, cols].astype(F32) + gbuf[:, cols].astype(F32)).astype(BF16)
         part[...] = jnp.zeros((ROWS, RANK), F32)
 
         def choose(i, carry):
@@ -349,7 +358,7 @@
             acc = jnp.zeros((ROWS, v.shape[0]), F32)
             for j in range(PARTS):
                 got = lax.dot_general(
-                    bbuf[:, j * PC:(j + 1) * PC], v, (((1,), (1,)), ((), ())), preferred_element_type=F32
+                    b_ref[:, j * PC:(j + 1) * PC], v, (((1,), (1,)), ((), ())), preferred_element_type=F32
                 )
                 acc = jnp.where(piece_of == j, got, acc)
             total = part[...]
@@ -387,16 +396,17 @@
     c3 = exchange(lambda p: gpart.at[tile(p)], lambda p: ybuf.at[p], y_id, y, ys, yr)
     ybuf[y] = gpart[tile(y)]
 
-    split = thirds(pv)
-    for j in range(7):
-        cols = slice(j * 512, (j + 1) * 512)
-        total = jnp.zeros((512, RANK), F32)
+    split = thirds(pv)[:2]
+    for j in range(PARTS):
+        cols = slice(j * PC, (j + 1) * PC)
+        total = jnp.zeros((PC, RANK), F32)
         for a in split[::-1]:
             total = total + lax.dot_general(
-                bbuf[:, cols], a, (((0,), (0,)), ((), ())), preferred_element_type=F32
+                b_ref[:, cols], a, (((0,), (0,)), ((), ())), preferred_element_type=F32
             )
-        work[cols, :] = total
-    cut = lambda ax, origin, i: pl.ds(pl.multiple_of(slot_of(ax, origin, i) * CUT, 8), CUT)
+        for i in range(16):
+            work[(j * 16 + i) * PACK:(j * 16 + i + 1) * PACK, :] = pack(total[i * CUT:(i + 1) * CUT, :])
+    cut = lambda ax, origin, i: pl.ds(pl.multiple_of(slot_of(ax, origin, i) * PACK, 16), PACK)
     streams = [(ax, d, i) for i in range(4) for ax in range(2) for d in range(2)]
     hops = lambda d, i: 4 if fourth(d, i) else 3
     sent = []
@@ -422,7 +432,8 @@
                 came(ax, d, i, h)
                 if h + 1 < n:
                     step = 1 if d == 0 else -1
-                    land[ax, d, i, h] = land[ax, d, i, h] + work[cut(ax, mod8(at[ax] + step * (n - h - 1)), i), :]
+                    own = work[cut(ax, mod8(at[ax] + step * (n - h - 1)), i), :].astype(F32)
+                    land[ax, d, i, h] = (land[ax, d, i, h].astype(F32) + own).astype(BF16)
                     pass_on(ax, d, i, h + 1, land.at[ax, d, i, h])
 
     for ax, d, i in streams:
@@ -462,10 +473,10 @@
 
     for ax in range(2):
         for i in range(4):
-            both = work[cut(ax, at[ax], i), :]
+            both = work[cut(ax, at[ax], i), :].astype(F32)
             for d in range(2):
-                both = both + land[ax, d, i, hops(d, i) - 1]
-            near[ax, i] = both
+                both = both + land[ax, d, i, hops(d, i) - 1].astype(F32)
+            near[ax, i] = both.astype(BF16)
             to = target(ax, i)
 
             @pl.when(to != at[1 - ax])
@@ -474,7 +485,7 @@
 
             @pl.when(to == at[1 - ax])
             def _():
-                far[at[1 - ax]] = both
+                far[at[1 - ax]] = both.astype(BF16)
 
     arrived(lambda p: gram_ref.at[block(p)], tp_id, t, ts, tr)
     start_inverse(gram_ref[...], sx)
@@ -483,22 +494,21 @@
         step_inverse(sx)
         return carry
 
-    lax.fori_loop(0, 6, advance, 0)
-    err_ref[...] = missed(sx)
+    lax.fori_loop(0, 5, advance, 0)
+    check_ref[0] = missed(sx)
     for k in range(1, 8):
         p = mod8(spot + k)
         pltpu.make_async_remote_copy(
             src_ref=far.at[p], dst_ref=far.at[p], send_sem=s4.at[0, 0], recv_sem=r4.at[p],
             device_id=aside, device_id_type=MESH,
         ).wait_recv()
-    sums = far[0]
+    sums = far[0].astype(F32)
     for p in range(1, 8):
-        sums = sums + far[p]
-    z_ref[...] = sums
+        sums = sums + far[p].astype(F32)
+    zown = jnp.concatenate([sums[:CUT], sums[CUT:]], axis=1)
     sems = (s5, r5, s6, r6, e1, f1, e2, f2, e3, f3)
     spread(
-        sums, lambda: sx[:, RANK:], lambda: proj_ref[...], low_ref, back_ref, sq_ref, (f, t, y, z, even), q1, q2, q3, sems,
-        lambda: None,
+        zown, sx, proj_ref, check_ref, low_ref, back_ref, sq_ref, (f, t, y, z, even), q1, q2, q3, sems
     )
     finish()
     for copies in (c1, c2, c3, c4, c5, c6, sent):
@@ -511,20 +521,10 @@
                 cross(ax, i, aside).wait_send()
 
 
-def again_kernel(
-    proj_ref, x_ref, z_ref, low_ref, back_ref, sq_ref, q1, q2, q3, s1, r1, s2, r2, e1, f1, e2, f2, e3, f3
-):
-    where = place()
-    greet(*where[:4])
-    sems = (s1, r1, s2, r2, e1, f1, e2, f2, e3, f3)
-    spread(
-        z_ref[...], lambda: x_ref[...], lambda: proj_ref[...], low_ref, back_ref, sq_ref, where, q1, q2, q3, sems, met
-    )
-
-
-def output_kernel(m_ref, g_ref, low_ref, back_ref, sq_ref, mom_ref, own_ref, upd_ref):
+def output_kernel(b_ref, low_ref, back_ref, sq_ref, mom_ref, own_ref, upd_ref, mbuf, ubuf, sem):
     f = lax.axis_index("fsdp")
     squares = sq_ref[0:1, :] + epsilon
+    inverse = lax.rsqrt(squares)
     low = low_ref[...]
     scaled = (low.astype(F32) * jnp.sqrt(squares).astype(BF16).astype(F32)).astype(BF16)
     pick = jnp.where(
@@ -532,26 +532,39 @@
         1.0, 0.0,
     ).astype(BF16)
     turn = (((1,), (1,)), ((), ()))
-    pieces = [back_ref[s * PAD:s * PAD + CUT, :].astype(F32) for s in range(16)]
-    nb = (jnp.concatenate(pieces, axis=0) * lax.rsqrt(squares)).astype(BF16)
-    buffer = (m_ref[...].astype(F32) + g_ref[...].astype(F32)).astype(BF16).astype(F32)
-    own_ref[...] = lax.dot_general(pick, nb, turn, preferred_element_type=F32)[0:OWN].astype(BF16)
-    upd_ref[...] = (UNIT * lax.dot_general(low, nb, turn, preferred_element_type=F32)).astype(BF16)
-    mom_ref[...] = (
-        buffer - (1.0 - momentum_decay) * lax.dot_general(scaled, nb, turn, preferred_element_type=F32)
-    ).astype(BF16)
+    copies = []
+    for j in range(PARTS):
+        cols = slice(j * PC, (j + 1) * PC)
+        halves = [
+            jnp.concatenate(
+                [
+                    back_ref[s * PACK + h * CUT:s * PACK + (h + 1) * CUT, :].astype(F32)
+                    for s in range(j * 16, (j + 1) * 16)
+                ],
+                axis=0,
+            )
+            for h in range(2)
+        ]
+        nb = (jnp.concatenate(halves, axis=1) * inverse).astype(BF16)
+        own_ref[:, cols] = lax.dot_general(pick, nb, turn, preferred_element_type=F32)[0:OWN].astype(BF16)
+        ubuf[:, cols] = (UNIT * lax.dot_general(low, nb, turn, preferred_element_type=F32)).astype(BF16)
+        mbuf[:, cols] = (
+            b_ref[:, cols].astype(F32)
+            - (1.0 - momentum_decay) * lax.dot_general(scaled, nb, turn, preferred_element_type=F32)
+        ).astype(BF16)
+        for n, (src, dst) in enumerate(((ubuf, upd_ref), (mbuf, mom_ref))):
+            copy = pltpu.make_async_copy(src.at[:, cols], dst.at[:, cols], sem.at[n, j])
+            copy.start()
+            copies.append(copy)
+    for copy in copies:
+        copy.wait()
 
 
 VMEM = pl.BlockSpec(memory_space=pltpu.VMEM)
 HBM = pl.BlockSpec(memory_space=pltpu.HBM)
 DMA = pltpu.SemaphoreType.DMA
-LIMIT = 56 * 2**20
+LIMIT = 44 * 2**20
 WIDE = (2, 2, 4, 4)
-SPREAD = [
-    jax.ShapeDtypeStruct((ROWS, RANK), BF16),
-    jax.ShapeDtypeStruct((NF * PAD, RANK), BF16),
-    jax.ShapeDtypeStruct((8, RANK), F32),
-]
 
 
 def project(momentum, gradient, basis_rows):
@@ -560,14 +573,16 @@
         out_shape=[
             jax.ShapeDtypeStruct((ROWS, RANK), F32),
             jax.ShapeDtypeStruct((RANK, RANK), F32),
-            jax.ShapeDtypeStruct((CUT, RANK), F32),
-            jax.ShapeDtypeStruct((1, RANK), F32),
-        ] + SPREAD,
+            jax.ShapeDtypeStruct((2,), F32),
+            jax.ShapeDtypeStruct((ROWS, COLS), BF16),
+            jax.ShapeDtypeStruct((ROWS, RANK), BF16),
+            jax.ShapeDtypeStruct((NF * PACK, HALF), BF16),
+            jax.ShapeDtypeStruct((8, RANK), F32),
+        ],
         in_specs=[HBM, HBM, HBM],
-        out_specs=[VMEM] * 7,
+        out_specs=[VMEM, VMEM, pl.BlockSpec(memory_space=pltpu.SMEM), VMEM, VMEM, VMEM, VMEM],
         scratch_shapes=[
             pltpu.VMEM((NF * SLOT, PC), BF16),
-            pltpu.VMEM((ROWS, COLS), BF16),
             pltpu.VMEM((ROWS, COLS), BF16),
             pltpu.VMEM((ROWS, COLS), BF16),
             pltpu.VMEM((OWN, COLS), BF16),
@@ -577,10 +592,10 @@
             pltpu.VMEM((RANK, RANK), F32),
             pltpu.VMEM((8, 8, 128), F32),
             pltpu.VMEM((8, 8, 128), F32),
-            pltpu.VMEM((COLS, RANK), F32),
-            pltpu.VMEM(WIDE + (CUT, RANK), F32),
-            pltpu.VMEM((2, 4, CUT, RANK), F32),
-            pltpu.VMEM((8, CUT, RANK), F32),
+            pltpu.VMEM((NF * PACK, HALF), BF16),
+            pltpu.VMEM(WIDE + (PACK, HALF), BF16),
+            pltpu.VMEM((2, 4, PACK, HALF), BF16),
+            pltpu.VMEM((8, PACK, HALF), BF16),
             pltpu.VMEM((RANK, 2 * RANK), F32),
             pltpu.VMEM((8, 8, RANK), F32),
             pltpu.VMEM((8, 8, RANK), F32),
@@ -594,22 +609,7 @@
     )(momentum, gradient, basis_rows)
 
 
-def again(proj, x, zown):
-    return pl.pallas_call(
-        again_kernel,
-        out_shape=SPREAD,
-        in_specs=[VMEM] * 3,
-        out_specs=[VMEM] * 3,
-        scratch_shapes=[pltpu.VMEM((8, 8, RANK), F32)] * 3
-        + [DMA((8,)), DMA((8,)), DMA(WIDE), DMA(WIDE)]
-        + [DMA((8,))] * 6,
-        compiler_params=pltpu.CompilerParams(collective_id=1, has_side_effects=True, vmem_limit_bytes=LIMIT),
-        name="again",
-    )(proj, x, zown)
-
-
-def outputs(momentum, gradient, low, back, squares):
-    tall = pl.BlockSpec((ROWS, PC), lambda j: (0, j))
+def outputs(buffer, low, back, squares):
     return pl.pallas_call(
         output_kernel,
         out_shape=[
@@ -617,34 +617,35 @@
             jax.ShapeDtypeStruct((OWN, COLS), BF16),
             jax.ShapeDtypeStruct((ROWS, COLS), BF16),
         ],
-        grid=(PARTS,),
-        in_specs=[
-            tall,
-            tall,
-            pl.BlockSpec((ROWS, RANK), lambda j: (0, 0)),
-            pl.BlockSpec((16 * PAD, RANK), lambda j: (j, 0)),
-            pl.BlockSpec((8, RANK), lambda j: (0, 0)),
-        ],
-        out_specs=[tall, pl.BlockSpec((OWN, PC), lambda j: (0, j)), tall],
-        compiler_params=pltpu.CompilerParams(vmem_limit_bytes=LIMIT),
+        in_specs=[VMEM] * 4,
+        out_specs=[HBM, VMEM, HBM],
+        scratch_shapes=[pltpu.VMEM((ROWS, COLS), BF16)] * 2 + [DMA((2, PARTS))],
+        compiler_params=pltpu.CompilerParams(vmem_limit_bytes=32 * 2**20),
         name="outputs",
-    )(momentum, gradient, low, back, squares)
-
-
-def direct(gram):
+    )(buffer, low, back, squares)
+
+
+def direct(proj, gram, buffer):
     lower_factor = jnp.linalg.cholesky(gram)
-    return lax.linalg.triangular_solve(lower_factor, jnp.eye(RANK, dtype=F32), left_side=True, lower=True)
+    low = lax.linalg.triangular_solve(
+        lower_factor, proj, left_side=False, lower=True, transpose_a=True
+    ).astype(BF16)
+    back = lax.psum(
+        lax.dot_general(low, buffer, (((0,), (0,)), ((), ())), preferred_element_type=F32), "fsdp"
+    )
+    squares = lax.psum(jnp.sum(back * back, axis=1), "tp")
+    packed = back.T.reshape(NF, CUT, 2, HALF).transpose(0, 2, 1, 3).reshape(NF * PACK, HALF)
+    return low, packed.astype(BF16), jnp.broadcast_to(squares[None, :], (8, RANK))
 
 
 def local(momentum, gradient, basis_rows):
-    proj, gram, zown, err, low, back, squares = project(momentum, gradient, basis_rows)
-    low, back, squares = lax.cond(
-        jnp.sum(err) < 1e-8,
-        lambda proj, gram, zown, *now: now,
-        lambda proj, gram, zown, *now: tuple(again(proj, direct(gram), zown)),
-        proj, gram, zown, low, back, squares,
-    )
-    return tuple(outputs(momentum, gradient, low, back, squares))
+    proj, gram, check, buffer, low, back, squares = project(momentum, gradient, basis_rows)
+    return lax.cond(
+        jnp.logical_and(check[0] < 1e-8, check[1] < 4.0),
+        lambda proj, gram, buffer, *now: tuple(outputs(buffer, *now)),
+        lambda proj, gram, buffer, *now: tuple(outputs(buffer, *direct(proj, gram, buffer))),
+        proj, gram, buffer, low, back, squares,
+    )
 
 
 def solution(mesh):

time: 207 us -> 373 us (1.80)
  waiting for transfers between devices: 0 us -> 164 us
  Pallas kernels: 138 us -> 97.6 us
  blocking collectives: 0 us -> 16.3 us
  between operations: 1.3 us -> 15.4 us
  local copies, waits for them, and re-layouts: 4.28 us -> 14.1 us
    psum x0 -> x1, waiting for transfers between devices: none -> 164 us  [direct(): lax.psum(lax.dot_general(low, buffer, (((0,), (0,)), ((), ())), preferred...]
    pallas_call x1 -> x0, Pallas kernels: 29.5 us -> none  [again(): pl.pallas_call(again_kernel, out_shape=SPREAD, in_specs=[VMEM] * 3, out_s...]
    psum x0 -> x1, blocking collectives: none -> 16.3 us  [direct(): squares = lax.psum(jnp.sum(back * back, axis=1), 'tp')]
    pallas_call x1, Pallas kernels: 104 us -> 94.5 us  [project(): pl.pallas_call(project_kernel, out_shape=[jax.ShapeDtypeStruct((ROWS, RAN...]
    convert_element_type x0 -> x3, local copies, waits for them, and re-layouts: none -> 6.12 us  [direct(): packed.astype(BF16)]
  transfers between devices with their start and end apart: 0 -> 1, of which waited for: 0 -> 1; matrix products, arithmetic and copies ran while one was open for 0% -> 0% of each run, Pallas kernels for 0% -> 0%
where the time goes in v4:
time: 373 us; the launch traced here: 372 us
  waiting for transfers between devices  164 us (44%)
  Pallas kernels  97.6 us (26%)
  other arithmetic  58.5 us (16%)
  blocking collectives  16.3 us (4%)
  between operations  15.4 us (4%)
  local copies, waits for them, and re-layouts  14.1 us (4%)
  matrix products  3.75 us (1%)
    psum x1, waiting for transfers between devices, direct(): lax.psum(lax.dot_general(low, buffer, (((0,), (0,)), ((), ())), preferred...  164 us
    pallas_call x1, Pallas kernels, project(): pl.pallas_call(project_kernel, out_shape=[jax.ShapeDtypeStruct((ROWS, RAN...  94.5 us
    another operation x6, other arithmetic, direct(): lower_factor = jnp.linalg.cholesky(gram)  34 us
    another operation x4, other arithmetic, direct(): lax.linalg.triangular_solve(lower_factor, proj, left_side=False, lower=Tr...  19.7 us
    psum x1, blocking collectives, direct(): squares = lax.psum(jnp.sum(back * back, axis=1), 'tp')  16.3 us
  transfers between devices with their start and end apart: 1, of which 1 were waited for; matrix products, arithmetic and copies ran while one was open for 0% of the time, Pallas kernels for 0%

profile of v4, /device:TPU:1, one launch (start us, length us, event | category | flops | bytes accessed | tf_op | source)
XLA Modules:
  0.0 372.2 jit_solution(2306556641342842630)
XLA Ops:
  7.2 1.2 copy-done
  8.3 1.2 copy-done.1
  9.5 0.7 copy-done.2
  10.3 94.5 %project.1 = (f32[128,256]{1,0:T(8,128)S(1)}, f32[256,256]{1,0:T(8,128)S(1)}, f32[2]{0:T(128)S(1)}, bf16[128,3584]{1,0:T(8,128)(2,1)S(1)}, bf16[128,256]{1,0:T(8...) custom-call(bf16[128,3584]{1,0:T(8,128)(2,1)S(1)} %copy-done, bf16[128,3584]{1,0:T(8,128)(2,1)S(1)} %copy-done.1, ...), custom_call_target="tpu_custom_call" | custom-call | tf_op jit(solution)/shard_map/project/pallas_call | solution.py:571
  104.8 0.6 fusion.9
  106.7 258.6 %conditional.1 = ((bf16[128,3584]{1,0:T(8,128)(2,1)}, bf16[4,3584]{1,0:T(4,128)(2,1)}, bf16[128,3584]{1,0:T(8,128)(2,1)})) conditional(s32[]{:T(128)} %bitcast.9, (f32[256,256]{1,0:T(8,128)S(1)}, f32[128,256]{1,0:T(8,128)S(1)}, bf16[128,3584]{1,0:T(8,128)(2,1)S(1)}) %tuple.13, (bf16[128,3584]{1,0:T(8,128)(2,1)S(1)}, bf16[128,256]{1,0:T(8,128)(2,1)S(1)}, ...), branch_computations={%region_0.8_spmd, %region_8.9_spmd} | conditional | flops 365216000 | bytes 47266048 | solution.py:643
  106.7 0.2 all-reduce.3.cloned.1.call-start
  106.9 0.1 copy.22
  107.1 11.7 %cholesky.5 = f32[128,128]{1,0:T(8,128)S(1)} custom-call(f32[128,128]{1,0:T(8,128)S(1)} %cholesky.46), custom_call_target="Cholesky" | custom-call | tf_op jit(solution)/shard_map/cond/branch_0_fun/jit(cholesky)/cholesky | solution.py:629
  118.9 9.8 %custom-call.12 = f32[1,128,128]{1,2,0:T(8,128)S(1)} custom-call(f32[1,128,128]{2,1,0:T(8,128)S(1)} %get-tuple-element.76), custom_call_target="InvertDiagBlocksLowerTriangular" | custom-call | tf_op jit(solution)/shard_map/cond/branch_0_fun/jit(cholesky)/cholesky | solution.py:629
  128.7 0.2 constant_dynamic-update-slice_fusion.1
  128.9 0.3 convolution_subtract_fusion.1
  129.2 11.7 %cholesky.29 = f32[128,128]{1,0:T(8,128)S(1)} custom-call(f32[128,128]{1,0:T(8,128)S(1)} %convolution_subtract_fusion.1), custom_call_target="Cholesky" | custom-call | tf_op jit(solution)/shard_map/cond/branch_0_fun/jit(cholesky)/cholesky | solution.py:629
  141.0 0.6 compare_reduce_fusion
  143.0 4.2 %while.1 = (s32[]{:T(128)}, f32[256,256]{1,0:T(8,128)S(1)}, s32[2,2]{1,0:T(2,128)S(1)}, f32[2,128,128]{2,1,0:T(8,128)S(1)}, s32[]{:T(128)}) while((s32[]{:T(128)}, f32[256,256]{1,0:T(8,128)S(1)}, s32[2,2]{1,0:T(2,128)S(1)}, f32[2,128,128]{2,1,0:T(8,128)S(1)}, s32[]{:T(128)}) %tuple.43), condition=%wide.while_cond, body=%wide.while_body.sunk | while | flops 2 | bytes 131189 | solution.py:630
  143.2 0.6 fusion.16
  143.8 1.4 bitcast_dynamic-update-slice_fusion.2
  145.2 0.6 fusion.16
  145.8 1.4 bitcast_dynamic-update-slice_fusion.2
  147.2 19.7 %custom-call.13 = f32[2,128,128]{1,2,0:T(8,128)S(1)} custom-call(f32[2,128,128]{2,1,0:T(8,128)S(1)} %get-tuple-element.54), custom_call_target="InvertDiagBlocksLowerTriangular" | custom-call | tf_op jit(solution)/shard_map/cond/branch_0_fun/triangular_solve | solution.py:630
  166.9 0.3 fusion.2
  167.2 0.3 convolution_subtract_fusion
  167.5 0.1 copy.18
  167.6 0.2 convolution_convert_fusion
  167.8 2.5 fusion.7
  170.3 164.3 %all-reduce.3.cloned.1.call-done = f32[256,3584]{1,0:T(8,128)} async-done(((f32[256,3584]{1,0:T(8,128)}), f32[256,3584]{1,0:T(8,128)}) %all-reduce.3.cloned.1.call-update) | async-done | bytes 3670032 | tf_op jit(solution)/shard_map/cond/branch_0_fun/psum | solution.py:633
  334.7 4.8 %multiply_reduce_fusion = (f32[256]{0:T(256)S(1)}, bf16[3584,256]{0,1:T(8,128)(2,1)}) fusion(f32[256,3584]{1,0:T(8,128)} %all-reduce.3.cloned.1.call-done), kind=kLoop, calls=%fused_computation.2 | loop fusion | flops 2752256 | bytes 5506048 | tf_op jit(solution)/shard_map/cond/branch_0_fun/reduce_sum | solution.py:636
  339.5 16.3 %psum.13 = f32[256]{0:T(256)S(1)} all-reduce(f32[256]{0:T(256)S(1)} %get-tuple-element.71), channel_id=1, replica_groups=mesh['fsdp'=64,'tp'=8] {'tp'}, use_global_device_ids=true, to_apply=%region_7.7 | all-reduce | flops 256 | bytes 2048 | tf_op jit(solution)/shard_map/cond/branch_0_fun/psum | solution.py:636
  355.8 2.9 copy.20
  358.7 1.5 convert_element_type.6
  360.2 1.8 copy.21
  362.0 3.1 outputs.2
  (17 shorter events, 0.3 us)
Async XLA Ops:
  7.2 1.2 copy-start
  8.3 1.2 copy-start.1
  9.5 0.7 copy-start.2
  106.7 228.0 %all-reduce.3.cloned.1.call-start = ((), (), s32[]{:S(2)}) async-start(), calls=%async_computation | async-start | bytes 7340032 | tf_op jit(solution)/shard_map/cond/branch_0_fun/psum | solution.py:633
Sparse Core Ops, SparseCore 0:
  170.4 164.1 all-reduce.2

commit v5 on v4

--- a/solution.py
+++ b/solution.py
@@ -563,7 +563,7 @@
 VMEM = pl.BlockSpec(memory_space=pltpu.VMEM)
 HBM = pl.BlockSpec(memory_space=pltpu.HBM)
 DMA = pltpu.SemaphoreType.DMA
-LIMIT = 44 * 2**20
+LIMIT = 56 * 2**20
 WIDE = (2, 2, 4, 4)
 
 
@@ -625,15 +625,23 @@
     )(buffer, low, back, squares)
 
 
+def ring_sum(value, axis, n):
+    def step(_, state):
+        moving, total = state
+        moving = lax.ppermute(moving, axis, [(i, (i + 1) % n) for i in range(n)])
+        return moving, total + moving
+
+    return lax.fori_loop(0, n - 1, step, (value, value))[1]
+
+
 def direct(proj, gram, buffer):
     lower_factor = jnp.linalg.cholesky(gram)
     low = lax.linalg.triangular_solve(
         lower_factor, proj, left_side=False, lower=True, transpose_a=True
     ).astype(BF16)
-    back = lax.psum(
-        lax.dot_general(low, buffer, (((0,), (0,)), ((), ())), preferred_element_type=F32), "fsdp"
-    )
-    squares = lax.psum(jnp.sum(back * back, axis=1), "tp")
+    partial = lax.dot_general(low, buffer, (((0,), (0,)), ((), ())), preferred_element_type=F32)
+    back = ring_sum(partial, "fsdp", NF)
+    squares = ring_sum(jnp.sum(back * back, axis=1), "tp", NT)
     packed = back.T.reshape(NF, CUT, 2, HALF).transpose(0, 2, 1, 3).reshape(NF * PACK, HALF)
     return low, packed.astype(BF16), jnp.broadcast_to(squares[None, :], (8, RANK))
 

time: 373 us -> 5520 us (14.80)
  waiting for transfers between devices: 164 us -> 4580 us
  local copies, waits for them, and re-layouts: 14.1 us -> 396 us
  other arithmetic: 58.5 us -> 245 us
  starting transfers between devices: 0.22 us -> 184 us
    ppermute x0 -> x70, waiting for transfers between devices: none -> 4580 us  [step(): moving = lax.ppermute(moving, axis, [(i, (i + 1) % n) for i in range(n)])]
    while x0 -> x322, local copies, waits for them, and re-layouts: none -> 381 us
    add x0 -> x70, other arithmetic: none -> 187 us  [step(): return (moving, total + moving)]
    ppermute x0 -> x70, starting transfers between devices: none -> 184 us  [step(): moving = lax.ppermute(moving, axis, [(i, (i + 1) % n) for i in range(n)])]
    psum x1 -> x0, waiting for transfers between devices: 164 us -> none  [direct(): lax.psum(lax.dot_general(low, buffer, (((0,), (0,)), ((), ())), preferred...]
  transfers between devices with their start and end apart: 1 -> 70, of which waited for: 1 -> 70; matrix products, arithmetic and copies ran while one was open for 0% -> 0% of each run, Pallas kernels for 0% -> 0%
where the time goes in v5:
time: 5520 us; the launch traced here: 5510 us
  waiting for transfers between devices  4580 us (83%)
  local copies, waits for them, and re-layouts  396 us (7%)
  other arithmetic  245 us (4%)
  starting transfers between devices  184 us (3%)
  Pallas kernels  97 us (2%)
    ppermute x70, waiting for transfers between devices, step(): moving = lax.ppermute(moving, axis, [(i, (i + 1) % n) for i in range(n)])  4580 us
    while x322, local copies, waits for them, and re-layouts  381 us
    add x70, other arithmetic, step(): return (moving, total + moving)  187 us
    ppermute x70, starting transfers between devices, step(): moving = lax.ppermute(moving, axis, [(i, (i + 1) % n) for i in range(n)])  184 us
  transfers between devices with their start and end apart: 70, of which 70 were waited for; matrix products, arithmetic and copies ran while one was open for 0% of the time, Pallas kernels for 0%

profile of v5, /device:TPU:1, one launch (start us, length us, event | category | flops | bytes accessed | tf_op | source)
XLA Modules:
  0.0 5512.1 jit_solution(17752969163925780664)
XLA Ops:
  0.6 93.9 %project.1 = (f32[128,256]{1,0:T(8,128)S(1)}, f32[256,256]{1,0:T(8,128)S(1)}, f32[2]{0:T(128)}, bf16[128,3584]{1,0:T(8,128)(2,1)S(1)}, bf16[128,256]{1,0:T(8,128...) custom-call(bf16[128,3584]{1,0:T(8,128)(2,1)} %m_ref.1, bf16[128,3584]{1,0:T(8,128)(2,1)} %g_ref.1, ...), custom_call_target="tpu_custom_call" | custom-call | tf_op jit(solution)/shard_map/project/pallas_call | solution.py:571
  97.2 5414.7 %conditional.1 = ((bf16[128,3584]{1,0:T(8,128)(2,1)}, bf16[4,3584]{1,0:T(4,128)(2,1)}, bf16[128,3584]{1,0:T(8,128)(2,1)})) conditional(s32[]{:T(128)} %bitcast.9, (f32[256,256]{1,0:T(8,128)S(1)}, f32[128,256]{1,0:T(8,128)S(1)}, bf16[128,3584]{1,0:T(8,128)(2,1)S(1)}) %tuple.21, (bf16[128,3584]{1,0:T(8,128)(2,1)S(1)}, ...), branch_computations={%region_0.10_spmd, %region_10.11_spmd} | conditional | flops 365216000 | bytes 109665848 | solution.py:651
  162.0 5245.9 %while.23 = (s32[]{:T(128)}, f32[256,3584]{1,0:T(8,128)}, f32[256,3584]{1,0:T(8,128)}, s32[]{:T(128)}) while((s32[]{:T(128)}, f32[256,3584]{1,0:T(8,128)}, f32[256,3584]{1,0:T(8,128)}, s32[]{:T(128)}) %tuple.80), condition=%wide.region_6.6_spmd, body=%wide.region_5.5_spmd.sunk | while | flops 917506 | bytes 62390420 | solution.py:634
  163.9 79.7 %collective-permute-done = f32[256,3584]{1,0:T(8,128)} collective-permute-done((f32[256,3584]{1,0:T(8,128)}, f32[256,3584]{1,0:T(8,128)}, u32[]{:S(2)}, u32[]{:S(2)}) %collective-permute-start) | collective-permute-done | bytes 3670048 | tf_op jit(solution)/shard_map/cond/branch_0_fun/while/body/eval_jaxpr/ppermute | solution.py:631
  254.5 78.8 %collective-permute-done = f32[256,3584]{1,0:T(8,128)} collective-permute-done((f32[256,3584]{1,0:T(8,128)}, f32[256,3584]{1,0:T(8,128)}, u32[]{:S(2)}, u32[]{:S(2)}) %collective-permute-start) | collective-permute-done | bytes 3670048 | tf_op jit(solution)/shard_map/cond/branch_0_fun/while/body/eval_jaxpr/ppermute | solution.py:631
  344.3 77.9 %collective-permute-done = f32[256,3584]{1,0:T(8,128)} collective-permute-done((f32[256,3584]{1,0:T(8,128)}, f32[256,3584]{1,0:T(8,128)}, u32[]{:S(2)}, u32[]{:S(2)}) %collective-permute-start) | collective-permute-done | bytes 3670048 | tf_op jit(solution)/shard_map/cond/branch_0_fun/while/body/eval_jaxpr/ppermute | solution.py:631
  433.1 76.9 %collective-permute-done = f32[256,3584]{1,0:T(8,128)} collective-permute-done((f32[256,3584]{1,0:T(8,128)}, f32[256,3584]{1,0:T(8,128)}, u32[]{:S(2)}, u32[]{:S(2)}) %collective-permute-start) | collective-permute-done | bytes 3670048 | tf_op jit(solution)/shard_map/cond/branch_0_fun/while/body/eval_jaxpr/ppermute | solution.py:631
  521.0 76.0 %collective-permute-done = f32[256,3584]{1,0:T(8,128)} collective-permute-done((f32[256,3584]{1,0:T(8,128)}, f32[256,3584]{1,0:T(8,128)}, u32[]{:S(2)}, u32[]{:S(2)}) %collective-permute-start) | collective-permute-done | bytes 3670048 | tf_op jit(solution)/shard_map/cond/branch_0_fun/while/body/eval_jaxpr/ppermute | solution.py:631
  607.9 75.1 %collective-permute-done = f32[256,3584]{1,0:T(8,128)} collective-permute-done((f32[256,3584]{1,0:T(8,128)}, f32[256,3584]{1,0:T(8,128)}, u32[]{:S(2)}, u32[]{:S(2)}) %collective-permute-start) | collective-permute-done | bytes 3670048 | tf_op jit(solution)/shard_map/cond/branch_0_fun/while/body/eval_jaxpr/ppermute | solution.py:631
  694.0 74.2 %collective-permute-done = f32[256,3584]{1,0:T(8,128)} collective-permute-done((f32[256,3584]{1,0:T(8,128)}, f32[256,3584]{1,0:T(8,128)}, u32[]{:S(2)}, u32[]{:S(2)}) %collective-permute-start) | collective-permute-done | bytes 3670048 | tf_op jit(solution)/shard_map/cond/branch_0_fun/while/body/eval_jaxpr/ppermute | solution.py:631
  779.1 73.3 %collective-permute-done = f32[256,3584]{1,0:T(8,128)} collective-permute-done((f32[256,3584]{1,0:T(8,128)}, f32[256,3584]{1,0:T(8,128)}, u32[]{:S(2)}, u32[]{:S(2)}) %collective-permute-start) | collective-permute-done | bytes 3670048 | tf_op jit(solution)/shard_map/cond/branch_0_fun/while/body/eval_jaxpr/ppermute | solution.py:631
  863.3 72.3 %collective-permute-done = f32[256,3584]{1,0:T(8,128)} collective-permute-done((f32[256,3584]{1,0:T(8,128)}, f32[256,3584]{1,0:T(8,128)}, u32[]{:S(2)}, u32[]{:S(2)}) %collective-permute-start) | collective-permute-done | bytes 3670048 | tf_op jit(solution)/shard_map/cond/branch_0_fun/while/body/eval_jaxpr/ppermute | solution.py:631
  3693.0 72.1 %collective-permute-done = f32[256,3584]{1,0:T(8,128)} collective-permute-done((f32[256,3584]{1,0:T(8,128)}, f32[256,3584]{1,0:T(8,128)}, u32[]{:S(2)}, u32[]{:S(2)}) %collective-permute-start) | collective-permute-done | bytes 3670048 | tf_op jit(solution)/shard_map/cond/branch_0_fun/while/body/eval_jaxpr/ppermute | solution.py:631
  3776.1 73.2 %collective-permute-done = f32[256,3584]{1,0:T(8,128)} collective-permute-done((f32[256,3584]{1,0:T(8,128)}, f32[256,3584]{1,0:T(8,128)}, u32[]{:S(2)}, u32[]{:S(2)}) %collective-permute-start) | collective-permute-done | bytes 3670048 | tf_op jit(solution)/shard_map/cond/branch_0_fun/while/body/eval_jaxpr/ppermute | solution.py:631
  3860.2 74.3 %collective-permute-done = f32[256,3584]{1,0:T(8,128)} collective-permute-done((f32[256,3584]{1,0:T(8,128)}, f32[256,3584]{1,0:T(8,128)}, u32[]{:S(2)}, u32[]{:S(2)}) %collective-permute-start) | collective-permute-done | bytes 3670048 | tf_op jit(solution)/shard_map/cond/branch_0_fun/while/body/eval_jaxpr/ppermute | solution.py:631
  3945.4 75.3 %collective-permute-done = f32[256,3584]{1,0:T(8,128)} collective-permute-done((f32[256,3584]{1,0:T(8,128)}, f32[256,3584]{1,0:T(8,128)}, u32[]{:S(2)}, u32[]{:S(2)}) %collective-permute-start) | collective-permute-done | bytes 3670048 | tf_op jit(solution)/shard_map/cond/branch_0_fun/while/body/eval_jaxpr/ppermute | solution.py:631
  4031.7 76.4 %collective-permute-done = f32[256,3584]{1,0:T(8,128)} collective-permute-done((f32[256,3584]{1,0:T(8,128)}, f32[256,3584]{1,0:T(8,128)}, u32[]{:S(2)}, u32[]{:S(2)}) %collective-permute-start) | collective-permute-done | bytes 3670048 | tf_op jit(solution)/shard_map/cond/branch_0_fun/while/body/eval_jaxpr/ppermute | solution.py:631
  4119.1 77.5 %collective-permute-done = f32[256,3584]{1,0:T(8,128)} collective-permute-done((f32[256,3584]{1,0:T(8,128)}, f32[256,3584]{1,0:T(8,128)}, u32[]{:S(2)}, u32[]{:S(2)}) %collective-permute-start) | collective-permute-done | bytes 3670048 | tf_op jit(solution)/shard_map/cond/branch_0_fun/while/body/eval_jaxpr/ppermute | solution.py:631
  4207.6 78.6 %collective-permute-done = f32[256,3584]{1,0:T(8,128)} collective-permute-done((f32[256,3584]{1,0:T(8,128)}, f32[256,3584]{1,0:T(8,128)}, u32[]{:S(2)}, u32[]{:S(2)}) %collective-permute-start) | collective-permute-done | bytes 3670048 | tf_op jit(solution)/shard_map/cond/branch_0_fun/while/body/eval_jaxpr/ppermute | solution.py:631
  4297.1 79.7 %collective-permute-done = f32[256,3584]{1,0:T(8,128)} collective-permute-done((f32[256,3584]{1,0:T(8,128)}, f32[256,3584]{1,0:T(8,128)}, u32[]{:S(2)}, u32[]{:S(2)}) %collective-permute-start) | collective-permute-done | bytes 3670048 | tf_op jit(solution)/shard_map/cond/branch_0_fun/while/body/eval_jaxpr/ppermute | solution.py:631
  4387.7 80.7 %collective-permute-done = f32[256,3584]{1,0:T(8,128)} collective-permute-done((f32[256,3584]{1,0:T(8,128)}, f32[256,3584]{1,0:T(8,128)}, u32[]{:S(2)}, u32[]{:S(2)}) %collective-permute-start) | collective-permute-done | bytes 3670048 | tf_op jit(solution)/shard_map/cond/branch_0_fun/while/body/eval_jaxpr/ppermute | solution.py:631
  4479.4 81.8 %collective-permute-done = f32[256,3584]{1,0:T(8,128)} collective-permute-done((f32[256,3584]{1,0:T(8,128)}, f32[256,3584]{1,0:T(8,128)}, u32[]{:S(2)}, u32[]{:S(2)}) %collective-permute-start) | collective-permute-done | bytes 3670048 | tf_op jit(solution)/shard_map/cond/branch_0_fun/while/body/eval_jaxpr/ppermute | solution.py:631
  4572.2 82.9 %collective-permute-done = f32[256,3584]{1,0:T(8,128)} collective-permute-done((f32[256,3584]{1,0:T(8,128)}, f32[256,3584]{1,0:T(8,128)}, u32[]{:S(2)}, u32[]{:S(2)}) %collective-permute-start) | collective-permute-done | bytes 3670048 | tf_op jit(solution)/shard_map/cond/branch_0_fun/while/body/eval_jaxpr/ppermute | solution.py:631
  4666.1 84.0 %collective-permute-done = f32[256,3584]{1,0:T(8,128)} collective-permute-done((f32[256,3584]{1,0:T(8,128)}, f32[256,3584]{1,0:T(8,128)}, u32[]{:S(2)}, u32[]{:S(2)}) %collective-permute-start) | collective-permute-done | bytes 3670048 | tf_op jit(solution)/shard_map/cond/branch_0_fun/while/body/eval_jaxpr/ppermute | solution.py:631
  4761.0 84.5 %collective-permute-done = f32[256,3584]{1,0:T(8,128)} collective-permute-done((f32[256,3584]{1,0:T(8,128)}, f32[256,3584]{1,0:T(8,128)}, u32[]{:S(2)}, u32[]{:S(2)}) %collective-permute-start) | collective-permute-done | bytes 3670048 | tf_op jit(solution)/shard_map/cond/branch_0_fun/while/body/eval_jaxpr/ppermute | solution.py:631
  4856.4 83.6 %collective-permute-done = f32[256,3584]{1,0:T(8,128)} collective-permute-done((f32[256,3584]{1,0:T(8,128)}, f32[256,3584]{1,0:T(8,128)}, u32[]{:S(2)}, u32[]{:S(2)}) %collective-permute-start) | collective-permute-done | bytes 3670048 | tf_op jit(solution)/shard_map/cond/branch_0_fun/while/body/eval_jaxpr/ppermute | solution.py:631
  4950.9 82.7 %collective-permute-done = f32[256,3584]{1,0:T(8,128)} collective-permute-done((f32[256,3584]{1,0:T(8,128)}, f32[256,3584]{1,0:T(8,128)}, u32[]{:S(2)}, u32[]{:S(2)}) %collective-permute-start) | collective-permute-done | bytes 3670048 | tf_op jit(solution)/shard_map/cond/branch_0_fun/while/body/eval_jaxpr/ppermute | solution.py:631
  5044.6 81.7 %collective-permute-done = f32[256,3584]{1,0:T(8,128)} collective-permute-done((f32[256,3584]{1,0:T(8,128)}, f32[256,3584]{1,0:T(8,128)}, u32[]{:S(2)}, u32[]{:S(2)}) %collective-permute-start) | collective-permute-done | bytes 3670048 | tf_op jit(solution)/shard_map/cond/branch_0_fun/while/body/eval_jaxpr/ppermute | solution.py:631
  5137.2 80.8 %collective-permute-done = f32[256,3584]{1,0:T(8,128)} collective-permute-done((f32[256,3584]{1,0:T(8,128)}, f32[256,3584]{1,0:T(8,128)}, u32[]{:S(2)}, u32[]{:S(2)}) %collective-permute-start) | collective-permute-done | bytes 3670048 | tf_op jit(solution)/shard_map/cond/branch_0_fun/while/body/eval_jaxpr/ppermute | solution.py:631
  5229.0 79.9 %collective-permute-done = f32[256,3584]{1,0:T(8,128)} collective-permute-done((f32[256,3584]{1,0:T(8,128)}, f32[256,3584]{1,0:T(8,128)}, u32[]{:S(2)}, u32[]{:S(2)}) %collective-permute-start) | collective-permute-done | bytes 3670048 | tf_op jit(solution)/shard_map/cond/branch_0_fun/while/body/eval_jaxpr/ppermute | solution.py:631
  5319.8 79.0 %collective-permute-done = f32[256,3584]{1,0:T(8,128)} collective-permute-done((f32[256,3584]{1,0:T(8,128)}, f32[256,3584]{1,0:T(8,128)}, u32[]{:S(2)}, u32[]{:S(2)}) %collective-permute-start) | collective-permute-done | bytes 3670048 | tf_op jit(solution)/shard_map/cond/branch_0_fun/while/body/eval_jaxpr/ppermute | solution.py:631
  5418.8 89.8 %while.24 = (s32[]{:T(128)}, f32[256]{0:T(256)S(1)}, f32[256]{0:T(256)S(1)}, s32[]{:T(128)}) while((s32[]{:T(128)}, f32[256]{0:T(256)S(1)}, f32[256]{0:T(256)S(1)}, s32[]{:T(128)}) %tuple.73), condition=%wide.region_9.9_spmd, body=%wide.region_8.8_spmd.sunk | while | flops 258 | bytes 9309 | solution.py:634
  (545 shorter events, 3223.4 us)
Async XLA Ops:
  162.0 81.6 %collective-permute-start = (f32[256,3584]{1,0:T(8,128)}, f32[256,3584]{1,0:T(8,128)}, u32[]{:S(2)}, u32[]{:S(2)}) collective-permute-start(f32[256,3584]{1,0:T(8,128)} %get-tuple-element.216), channel_id=1, source_target_pairs={{0,8},{8,16},{16,24},{24,32},{32,40},{40,48},{48,56},{56,64},{64,7... | collective-permute-start | bytes 11010056 | tf_op jit(solution)/shard_map/cond/branch_0_fun/while/body/eval_jaxpr/ppermute | solution.py:631
  252.6 80.7 %collective-permute-start = (f32[256,3584]{1,0:T(8,128)}, f32[256,3584]{1,0:T(8,128)}, u32[]{:S(2)}, u32[]{:S(2)}) collective-permute-start(f32[256,3584]{1,0:T(8,128)} %get-tuple-element.216), channel_id=1, source_target_pairs={{0,8},{8,16},{16,24},{24,32},{32,40},{40,48},{48,56},{56,64},{64,7... | collective-permute-start | bytes 11010056 | tf_op jit(solution)/shard_map/cond/branch_0_fun/while/body/eval_jaxpr/ppermute | solution.py:631
  342.4 79.8 %collective-permute-start = (f32[256,3584]{1,0:T(8,128)}, f32[256,3584]{1,0:T(8,128)}, u32[]{:S(2)}, u32[]{:S(2)}) collective-permute-start(f32[256,3584]{1,0:T(8,128)} %get-tuple-element.216), channel_id=1, source_target_pairs={{0,8},{8,16},{16,24},{24,32},{32,40},{40,48},{48,56},{56,64},{64,7... | collective-permute-start | bytes 11010056 | tf_op jit(solution)/shard_map/cond/branch_0_fun/while/body/eval_jaxpr/ppermute | solution.py:631
  431.2 78.9 %collective-permute-start = (f32[256,3584]{1,0:T(8,128)}, f32[256,3584]{1,0:T(8,128)}, u32[]{:S(2)}, u32[]{:S(2)}) collective-permute-start(f32[256,3584]{1,0:T(8,128)} %get-tuple-element.216), channel_id=1, source_target_pairs={{0,8},{8,16},{16,24},{24,32},{32,40},{40,48},{48,56},{56,64},{64,7... | collective-permute-start | bytes 11010056 | tf_op jit(solution)/shard_map/cond/branch_0_fun/while/body/eval_jaxpr/ppermute | solution.py:631
  519.0 77.9 %collective-permute-start = (f32[256,3584]{1,0:T(8,128)}, f32[256,3584]{1,0:T(8,128)}, u32[]{:S(2)}, u32[]{:S(2)}) collective-permute-start(f32[256,3584]{1,0:T(8,128)} %get-tuple-element.216), channel_id=1, source_target_pairs={{0,8},{8,16},{16,24},{24,32},{32,40},{40,48},{48,56},{56,64},{64,7... | collective-permute-start | bytes 11010056 | tf_op jit(solution)/shard_map/cond/branch_0_fun/while/body/eval_jaxpr/ppermute | solution.py:631
  606.0 77.0 %collective-permute-start = (f32[256,3584]{1,0:T(8,128)}, f32[256,3584]{1,0:T(8,128)}, u32[]{:S(2)}, u32[]{:S(2)}) collective-permute-start(f32[256,3584]{1,0:T(8,128)} %get-tuple-element.216), channel_id=1, source_target_pairs={{0,8},{8,16},{16,24},{24,32},{32,40},{40,48},{48,56},{56,64},{64,7... | collective-permute-start | bytes 11010056 | tf_op jit(solution)/shard_map/cond/branch_0_fun/while/body/eval_jaxpr/ppermute | solution.py:631
  692.1 76.1 %collective-permute-start = (f32[256,3584]{1,0:T(8,128)}, f32[256,3584]{1,0:T(8,128)}, u32[]{:S(2)}, u32[]{:S(2)}) collective-permute-start(f32[256,3584]{1,0:T(8,128)} %get-tuple-element.216), channel_id=1, source_target_pairs={{0,8},{8,16},{16,24},{24,32},{32,40},{40,48},{48,56},{56,64},{64,7... | collective-permute-start | bytes 11010056 | tf_op jit(solution)/shard_map/cond/branch_0_fun/while/body/eval_jaxpr/ppermute | solution.py:631
  777.2 75.2 %collective-permute-start = (f32[256,3584]{1,0:T(8,128)}, f32[256,3584]{1,0:T(8,128)}, u32[]{:S(2)}, u32[]{:S(2)}) collective-permute-start(f32[256,3584]{1,0:T(8,128)} %get-tuple-element.216), channel_id=1, source_target_pairs={{0,8},{8,16},{16,24},{24,32},{32,40},{40,48},{48,56},{56,64},{64,7... | collective-permute-start | bytes 11010056 | tf_op jit(solution)/shard_map/cond/branch_0_fun/while/body/eval_jaxpr/ppermute | solution.py:631
  861.4 74.3 %collective-permute-start = (f32[256,3584]{1,0:T(8,128)}, f32[256,3584]{1,0:T(8,128)}, u32[]{:S(2)}, u32[]{:S(2)}) collective-permute-start(f32[256,3584]{1,0:T(8,128)} %get-tuple-element.216), channel_id=1, source_target_pairs={{0,8},{8,16},{16,24},{24,32},{32,40},{40,48},{48,56},{56,64},{64,7... | collective-permute-start | bytes 11010056 | tf_op jit(solution)/shard_map/cond/branch_0_fun/while/body/eval_jaxpr/ppermute | solution.py:631
  944.7 73.3 %collective-permute-start = (f32[256,3584]{1,0:T(8,128)}, f32[256,3584]{1,0:T(8,128)}, u32[]{:S(2)}, u32[]{:S(2)}) collective-permute-start(f32[256,3584]{1,0:T(8,128)} %get-tuple-element.216), channel_id=1, source_target_pairs={{0,8},{8,16},{16,24},{24,32},{32,40},{40,48},{48,56},{56,64},{64,7... | collective-permute-start | bytes 11010056 | tf_op jit(solution)/shard_map/cond/branch_0_fun/while/body/eval_jaxpr/ppermute | solution.py:631
  1027.0 72.4 %collective-permute-start = (f32[256,3584]{1,0:T(8,128)}, f32[256,3584]{1,0:T(8,128)}, u32[]{:S(2)}, u32[]{:S(2)}) collective-permute-start(f32[256,3584]{1,0:T(8,128)} %get-tuple-element.216), channel_id=1, source_target_pairs={{0,8},{8,16},{16,24},{24,32},{32,40},{40,48},{48,56},{56,64},{64,7... | collective-permute-start | bytes 11010056 | tf_op jit(solution)/shard_map/cond/branch_0_fun/while/body/eval_jaxpr/ppermute | solution.py:631
  3528.2 71.9 %collective-permute-start = (f32[256,3584]{1,0:T(8,128)}, f32[256,3584]{1,0:T(8,128)}, u32[]{:S(2)}, u32[]{:S(2)}) collective-permute-start(f32[256,3584]{1,0:T(8,128)} %get-tuple-element.216), channel_id=1, source_target_pairs={{0,8},{8,16},{16,24},{24,32},{32,40},{40,48},{48,56},{56,64},{64,7... | collective-permute-start | bytes 11010056 | tf_op jit(solution)/shard_map/cond/branch_0_fun/while/body/eval_jaxpr/ppermute | solution.py:631
  3609.1 73.0 %collective-permute-start = (f32[256,3584]{1,0:T(8,128)}, f32[256,3584]{1,0:T(8,128)}, u32[]{:S(2)}, u32[]{:S(2)}) collective-permute-start(f32[256,3584]{1,0:T(8,128)} %get-tuple-element.216), channel_id=1, source_target_pairs={{0,8},{8,16},{16,24},{24,32},{32,40},{40,48},{48,56},{56,64},{64,7... | collective-permute-start | bytes 11010056 | tf_op jit(solution)/shard_map/cond/branch_0_fun/while/body/eval_jaxpr/ppermute | solution.py:631
  3691.1 74.0 %collective-permute-start = (f32[256,3584]{1,0:T(8,128)}, f32[256,3584]{1,0:T(8,128)}, u32[]{:S(2)}, u32[]{:S(2)}) collective-permute-start(f32[256,3584]{1,0:T(8,128)} %get-tuple-element.216), channel_id=1, source_target_pairs={{0,8},{8,16},{16,24},{24,32},{32,40},{40,48},{48,56},{56,64},{64,7... | collective-permute-start | bytes 11010056 | tf_op jit(solution)/shard_map/cond/branch_0_fun/while/body/eval_jaxpr/ppermute | solution.py:631
  3774.2 75.1 %collective-permute-start = (f32[256,3584]{1,0:T(8,128)}, f32[256,3584]{1,0:T(8,128)}, u32[]{:S(2)}, u32[]{:S(2)}) collective-permute-start(f32[256,3584]{1,0:T(8,128)} %get-tuple-element.216), channel_id=1, source_target_pairs={{0,8},{8,16},{16,24},{24,32},{32,40},{40,48},{48,56},{56,64},{64,7... | collective-permute-start | bytes 11010056 | tf_op jit(solution)/shard_map/cond/branch_0_fun/while/body/eval_jaxpr/ppermute | solution.py:631
  3858.3 76.2 %collective-permute-start = (f32[256,3584]{1,0:T(8,128)}, f32[256,3584]{1,0:T(8,128)}, u32[]{:S(2)}, u32[]{:S(2)}) collective-permute-start(f32[256,3584]{1,0:T(8,128)} %get-tuple-element.216), channel_id=1, source_target_pairs={{0,8},{8,16},{16,24},{24,32},{32,40},{40,48},{48,56},{56,64},{64,7... | collective-permute-start | bytes 11010056 | tf_op jit(solution)/shard_map/cond/branch_0_fun/while/body/eval_jaxpr/ppermute | solution.py:631
  3943.5 77.3 %collective-permute-start = (f32[256,3584]{1,0:T(8,128)}, f32[256,3584]{1,0:T(8,128)}, u32[]{:S(2)}, u32[]{:S(2)}) collective-permute-start(f32[256,3584]{1,0:T(8,128)} %get-tuple-element.216), channel_id=1, source_target_pairs={{0,8},{8,16},{16,24},{24,32},{32,40},{40,48},{48,56},{56,64},{64,7... | collective-permute-start | bytes 11010056 | tf_op jit(solution)/shard_map/cond/branch_0_fun/while/body/eval_jaxpr/ppermute | solution.py:631
  4029.8 78.4 %collective-permute-start = (f32[256,3584]{1,0:T(8,128)}, f32[256,3584]{1,0:T(8,128)}, u32[]{:S(2)}, u32[]{:S(2)}) collective-permute-start(f32[256,3584]{1,0:T(8,128)} %get-tuple-element.216), channel_id=1, source_target_pairs={{0,8},{8,16},{16,24},{24,32},{32,40},{40,48},{48,56},{56,64},{64,7... | collective-permute-start | bytes 11010056 | tf_op jit(solution)/shard_map/cond/branch_0_fun/while/body/eval_jaxpr/ppermute | solution.py:631
  4117.2 79.4 %collective-permute-start = (f32[256,3584]{1,0:T(8,128)}, f32[256,3584]{1,0:T(8,128)}, u32[]{:S(2)}, u32[]{:S(2)}) collective-permute-start(f32[256,3584]{1,0:T(8,128)} %get-tuple-element.216), channel_id=1, source_target_pairs={{0,8},{8,16},{16,24},{24,32},{32,40},{40,48},{48,56},{56,64},{64,7... | collective-permute-start | bytes 11010056 | tf_op jit(solution)/shard_map/cond/branch_0_fun/while/body/eval_jaxpr/ppermute | solution.py:631
  4205.6 80.5 %collective-permute-start = (f32[256,3584]{1,0:T(8,128)}, f32[256,3584]{1,0:T(8,128)}, u32[]{:S(2)}, u32[]{:S(2)}) collective-permute-start(f32[256,3584]{1,0:T(8,128)} %get-tuple-element.216), channel_id=1, source_target_pairs={{0,8},{8,16},{16,24},{24,32},{32,40},{40,48},{48,56},{56,64},{64,7... | collective-permute-start | bytes 11010056 | tf_op jit(solution)/shard_map/cond/branch_0_fun/while/body/eval_jaxpr/ppermute | solution.py:631
  4295.2 81.6 %collective-permute-start = (f32[256,3584]{1,0:T(8,128)}, f32[256,3584]{1,0:T(8,128)}, u32[]{:S(2)}, u32[]{:S(2)}) collective-permute-start(f32[256,3584]{1,0:T(8,128)} %get-tuple-element.216), channel_id=1, source_target_pairs={{0,8},{8,16},{16,24},{24,32},{32,40},{40,48},{48,56},{56,64},{64,7... | collective-permute-start | bytes 11010056 | tf_op jit(solution)/shard_map/cond/branch_0_fun/while/body/eval_jaxpr/ppermute | solution.py:631
  4385.8 82.7 %collective-permute-start = (f32[256,3584]{1,0:T(8,128)}, f32[256,3584]{1,0:T(8,128)}, u32[]{:S(2)}, u32[]{:S(2)}) collective-permute-start(f32[256,3584]{1,0:T(8,128)} %get-tuple-element.216), channel_id=1, source_target_pairs={{0,8},{8,16},{16,24},{24,32},{32,40},{40,48},{48,56},{56,64},{64,7... | collective-permute-start | bytes 11010056 | tf_op jit(solution)/shard_map/cond/branch_0_fun/while/body/eval_jaxpr/ppermute | solution.py:631
  4477.5 83.8 %collective-permute-start = (f32[256,3584]{1,0:T(8,128)}, f32[256,3584]{1,0:T(8,128)}, u32[]{:S(2)}, u32[]{:S(2)}) collective-permute-start(f32[256,3584]{1,0:T(8,128)} %get-tuple-element.216), channel_id=1, source_target_pairs={{0,8},{8,16},{16,24},{24,32},{32,40},{40,48},{48,56},{56,64},{64,7... | collective-permute-start | bytes 11010056 | tf_op jit(solution)/shard_map/cond/branch_0_fun/while/body/eval_jaxpr/ppermute | solution.py:631
  4570.3 84.8 %collective-permute-start = (f32[256,3584]{1,0:T(8,128)}, f32[256,3584]{1,0:T(8,128)}, u32[]{:S(2)}, u32[]{:S(2)}) collective-permute-start(f32[256,3584]{1,0:T(8,128)} %get-tuple-element.216), channel_id=1, source_target_pairs={{0,8},{8,16},{16,24},{24,32},{32,40},{40,48},{48,56},{56,64},{64,7... | collective-permute-start | bytes 11010056 | tf_op jit(solution)/shard_map/cond/branch_0_fun/while/body/eval_jaxpr/ppermute | solution.py:631
  4664.1 85.9 %collective-permute-start = (f32[256,3584]{1,0:T(8,128)}, f32[256,3584]{1,0:T(8,128)}, u32[]{:S(2)}, u32[]{:S(2)}) collective-permute-start(f32[256,3584]{1,0:T(8,128)} %get-tuple-element.216), channel_id=1, source_target_pairs={{0,8},{8,16},{16,24},{24,32},{32,40},{40,48},{48,56},{56,64},{64,7... | collective-permute-start | bytes 11010056 | tf_op jit(solution)/shard_map/cond/branch_0_fun/while/body/eval_jaxpr/ppermute | solution.py:631
  4759.1 86.4 %collective-permute-start = (f32[256,3584]{1,0:T(8,128)}, f32[256,3584]{1,0:T(8,128)}, u32[]{:S(2)}, u32[]{:S(2)}) collective-permute-start(f32[256,3584]{1,0:T(8,128)} %get-tuple-element.216), channel_id=1, source_target_pairs={{0,8},{8,16},{16,24},{24,32},{32,40},{40,48},{48,56},{56,64},{64,7... | collective-permute-start | bytes 11010056 | tf_op jit(solution)/shard_map/cond/branch_0_fun/while/body/eval_jaxpr/ppermute | solution.py:631
  4854.5 85.5 %collective-permute-start = (f32[256,3584]{1,0:T(8,128)}, f32[256,3584]{1,0:T(8,128)}, u32[]{:S(2)}, u32[]{:S(2)}) collective-permute-start(f32[256,3584]{1,0:T(8,128)} %get-tuple-element.216), channel_id=1, source_target_pairs={{0,8},{8,16},{16,24},{24,32},{32,40},{40,48},{48,56},{56,64},{64,7... | collective-permute-start | bytes 11010056 | tf_op jit(solution)/shard_map/cond/branch_0_fun/while/body/eval_jaxpr/ppermute | solution.py:631
  4949.0 84.6 %collective-permute-start = (f32[256,3584]{1,0:T(8,128)}, f32[256,3584]{1,0:T(8,128)}, u32[]{:S(2)}, u32[]{:S(2)}) collective-permute-start(f32[256,3584]{1,0:T(8,128)} %get-tuple-element.216), channel_id=1, source_target_pairs={{0,8},{8,16},{16,24},{24,32},{32,40},{40,48},{48,56},{56,64},{64,7... | collective-permute-start | bytes 11010056 | tf_op jit(solution)/shard_map/cond/branch_0_fun/while/body/eval_jaxpr/ppermute | solution.py:631
  5042.6 83.7 %collective-permute-start = (f32[256,3584]{1,0:T(8,128)}, f32[256,3584]{1,0:T(8,128)}, u32[]{:S(2)}, u32[]{:S(2)}) collective-permute-start(f32[256,3584]{1,0:T(8,128)} %get-tuple-element.216), channel_id=1, source_target_pairs={{0,8},{8,16},{16,24},{24,32},{32,40},{40,48},{48,56},{56,64},{64,7... | collective-permute-start | bytes 11010056 | tf_op jit(solution)/shard_map/cond/branch_0_fun/while/body/eval_jaxpr/ppermute | solution.py:631
  5135.3 82.7 %collective-permute-start = (f32[256,3584]{1,0:T(8,128)}, f32[256,3584]{1,0:T(8,128)}, u32[]{:S(2)}, u32[]{:S(2)}) collective-permute-start(f32[256,3584]{1,0:T(8,128)} %get-tuple-element.216), channel_id=1, source_target_pairs={{0,8},{8,16},{16,24},{24,32},{32,40},{40,48},{48,56},{56,64},{64,7... | collective-permute-start | bytes 11010056 | tf_op jit(solution)/shard_map/cond/branch_0_fun/while/body/eval_jaxpr/ppermute | solution.py:631
  5227.1 81.8 %collective-permute-start = (f32[256,3584]{1,0:T(8,128)}, f32[256,3584]{1,0:T(8,128)}, u32[]{:S(2)}, u32[]{:S(2)}) collective-permute-start(f32[256,3584]{1,0:T(8,128)} %get-tuple-element.216), channel_id=1, source_target_pairs={{0,8},{8,16},{16,24},{24,32},{32,40},{40,48},{48,56},{56,64},{64,7... | collective-permute-start | bytes 11010056 | tf_op jit(solution)/shard_map/cond/branch_0_fun/while/body/eval_jaxpr/ppermute | solution.py:631
  5317.9 80.9 %collective-permute-start = (f32[256,3584]{1,0:T(8,128)}, f32[256,3584]{1,0:T(8,128)}, u32[]{:S(2)}, u32[]{:S(2)}) collective-permute-start(f32[256,3584]{1,0:T(8,128)} %get-tuple-element.216), channel_id=1, source_target_pairs={{0,8},{8,16},{16,24},{24,32},{32,40},{40,48},{48,56},{56,64},{64,7... | collective-permute-start | bytes 11010056 | tf_op jit(solution)/shard_map/cond/branch_0_fun/while/body/eval_jaxpr/ppermute | solution.py:631
  (165 other events, 7170.8 us)
